TPU v7x, 128 devices: a whole 4x4x4 slice. The times are simulated.
128 devices in a mesh: ax: 8 (over x, core), az: 16 (over z, y).
Axes of the slice: x: 4, y: 4, z: 4, core: 2. Of those that a mesh axis runs over, the one named last changes fastest.
Arguments:
- state: float32 [4, 2, 16, 1024, 2048], P(None, None, None, 'az', 'ax'), as said below
- inflow: float32 [4, 2, 16, 1024], P(None, None, None, 'az'), as said below
- courant: float32 [16, 2048], P(None, 'ax'), may hold values from 1 to 12288
- mode_number: int32 [1024], P('az'), may hold values from 0 to 1023, as said below
- partner_table: int32 [1024], P('az'), may hold values from 0 to 1023, as said below
Outputs:
- new_state: float32 [4, 2, 16, 1024, 2048], P(None, None, None, 'az', 'ax')
Inputs may be any that keep to these rules, and one draw needn't show every extreme that they name: `mode_number`: a permutation of 0 .. 1023; where slot s < 512 holds k, slot s + 512 holds (1024 - k) mod 1024, except for one pair of slots s0 and s0 + 512 that hold 0 and 512. partner_table[s] = s at the two slots holding modes 0 and 512, and (s + 512) mod 1024 at all others. `state`: conjugate-symmetric over the slots: slot (s + 512) mod 1024 holds the complex conjugate of slot s, except at the two slots holding modes 0 and 512, whose imaginary parts are zero. `inflow`: conjugate-symmetric over the slots as state.
All inputs are finite; a program needn't handle non-finite values.
Results may differ from a plain program's by a relative error of at most 0.00012.
Values sent between devices are 32-bit elements; how exact they have to be, the bound alone decides.
A program may use at most 320 MiB of HBM per device.

v0:
```python
import math

import jax
import jax.numpy as jnp
from jax import lax
from jax.sharding import PartitionSpec as P

section_factor = 0.5
viscosity = 0.02


def extended(block, sides, width):
    for axis, dim in sides:
        count = lax.axis_size(axis)
        forward = [(i, i + 1) for i in range(count - 1)]
        backward = [(target, source) for source, target in forward]
        low = lax.ppermute(
            lax.slice_in_dim(block, block.shape[dim] - width, None, axis=dim), axis, forward
        )
        high = lax.ppermute(lax.slice_in_dim(block, 0, width, axis=dim), axis, backward)
        block = jnp.concatenate([low, block, high], axis=dim)
    return block


def from_behind(block, axis, distance):
    devices = range(lax.axis_size(axis))
    route = [(i - distance, i) for i in devices if i - distance in devices]
    return lax.ppermute(block, axis, route)


def contract(pattern, operand_a, operand_b):
    return jnp.einsum(pattern, operand_a, operand_b, precision=lax.Precision.HIGHEST)


def dft_tables(mode_ids, point_count):
    angles = jnp.arange(point_count, dtype=jnp.int32)
    phase_ids = mode_ids[:, None] * angles[None, :] % point_count
    angle_values = phase_ids.astype(jnp.float32) * (2.0 * math.pi / point_count)
    norm_factor = 1.0 / math.sqrt(point_count)
    return (jnp.cos(angle_values) * norm_factor, jnp.sin(angle_values) * norm_factor)


def signed_modes(mode_ids, point_count):
    half_count = point_count // 2
    shifted = jnp.where(mode_ids == half_count, 0, mode_ids - point_count)
    return jnp.where(mode_ids < half_count, mode_ids, shifted).astype(jnp.float32)


def radii(radial_ids, radial_count, point_count):
    return (
        point_count
        / (2.0 * math.pi)
        * (0.6 + 0.4 * (radial_ids.astype(jnp.float32) + 0.5) / radial_count)
    )


def untangle(spectrum, partner_vals, wave_ratio):
    ratio_wide = wave_ratio[None, :, :, None]
    real_terms = 0.5 * (spectrum[:, 0] + partner_vals[:, 0]) - 0.5 * ratio_wide * (
        spectrum[:, 0] - partner_vals[:, 0]
    )
    imag_terms = 0.5 * (spectrum[:, 1] - partner_vals[:, 1]) - 0.5 * ratio_wide * (
        spectrum[:, 1] + partner_vals[:, 1]
    )
    return jnp.stack([real_terms, imag_terms], axis=1)


def shards(state, inflow, courant, mode_number, partner_table):
    mode_all, partner_all = (
        lax.all_gather(mode_number, "az", axis=0, tiled=True),
        lax.all_gather(partner_table, "az", axis=0, tiled=True),
    )
    point_count = mode_all.shape[0]
    radial_count = state.shape[2]
    parts_az = lax.axis_size("az")
    local_radial = radial_count // parts_az
    cos_table, sin_table = dft_tables(mode_all, point_count)
    wavenumber_all = signed_modes(mode_all, point_count)
    wavenumber_local = signed_modes(mode_number, point_count)
    radial_ids = lax.axis_index("az") * local_radial + jnp.arange(local_radial, dtype=jnp.int32)
    local_inverse = 1.0 / radii(radial_ids, radial_count, point_count)
    all_inverse = 1.0 / radii(jnp.arange(radial_count, dtype=jnp.int32), radial_count, point_count)
    packed = jnp.stack(
        [
            state[0, 0] - state[1, 1],
            state[0, 1] + state[1, 0],
            state[2, 0] - state[3, 1],
            state[2, 1] + state[3, 0],
        ]
    )
    exchanged = lax.all_to_all(packed, "az", split_axis=1, concat_axis=2, tiled=True)
    real_parts = exchanged[0::2]
    imag_parts = exchanged[1::2]
    field_real = contract("prsx,sj->prjx", real_parts, cos_table) - contract(
        "prsx,sj->prjx", imag_parts, sin_table
    )
    field_imag = contract("prsx,sj->prjx", real_parts, sin_table) + contract(
        "prsx,sj->prjx", imag_parts, cos_table
    )
    fields = jnp.stack([field_real[0], field_imag[0], field_real[1], field_imag[1]])
    axial_flux = fields[0][None] * fields
    azim_flux = fields[2][None] * fields * local_inverse[None, :, None, None]
    padded = extended(axial_flux, (("ax", 3),), 1)
    divergence = -(padded[..., 2:] - padded[..., :-2]) * 0.5
    spec_real = contract("crjx,sj->crsx", divergence, cos_table) + contract(
        "crjx,sj->crsx", azim_flux, sin_table
    )
    spec_imag = contract("crjx,sj->crsx", azim_flux, cos_table) - contract(
        "crjx,sj->crsx", divergence, sin_table
    )
    spectra = jnp.stack([spec_real, spec_imag], axis=1)
    self_pair = (partner_all == jnp.arange(point_count, dtype=jnp.int32))[None, None, None, :, None]
    partner_vals = jnp.where(self_pair, spectra, jnp.roll(spectra, point_count // 2, axis=3))
    wave_ratio = wavenumber_all[None, :] * local_inverse[:, None]
    local_terms = untangle(spectra, partner_vals, wave_ratio)
    explicit_terms = lax.all_to_all(local_terms, "az", split_axis=3, concat_axis=2, tiled=True)
    ratio_local = wavenumber_local[None, :] * all_inverse[:, None]
    damping = viscosity * ratio_local * ratio_local
    section_input = state + section_factor * (
        explicit_terms - damping[None, None, :, :, None] * state
    )
    weight = courant / (1.0 + courant)
    log_cum = jnp.cumsum(jnp.log(weight), axis=1)
    log_gap = log_cum[:, None, :] - log_cum[:, :, None]
    cell_index = jnp.arange(weight.shape[1], dtype=jnp.int32)
    below_mask = cell_index[None, :, None] <= cell_index[None, None, :]
    transfer = jnp.where(
        below_mask, (1.0 - weight)[:, :, None] * jnp.exp(jnp.minimum(log_gap, 0.0)), 0.0
    )
    swept_cells = contract("cdrmj,rji->cdrmi", section_input, transfer)
    reach_decay = jnp.exp(log_cum)
    block_decay = reach_decay[:, -1]
    block_last = swept_cells[..., -1]
    first_device = lax.axis_index("ax") == 0
    decay_bcast = block_decay[None, None, :, None]

    def relay_turn(turn_index, incoming):
        outgoing = decay_bcast * incoming + block_last
        received = from_behind(outgoing, "ax", 1)
        return jnp.where(first_device, inflow, received)

    initial = jnp.where(first_device, inflow, jnp.zeros_like(inflow))
    incoming = lax.fori_loop(0, lax.axis_size("ax") - 1, relay_turn, initial)
    return swept_cells + reach_decay[None, None, :, None, :] * incoming[..., None]


def solution(mesh):
    in_specs = (
        P(None, None, None, "az", "ax"),
        P(None, None, None, "az"),
        P(None, "ax"),
        P("az"),
        P("az"),
    )
    out_specs = P(None, None, None, "az", "ax")
    return jax.shard_map(shards, mesh=mesh, in_specs=in_specs, out_specs=out_specs, check_vma=False)
```

profile of v0, /device:TPU:1, one launch (start us, length us, event | category | flops | bytes accessed | tf_op | source)
XLA Modules:
  0.0 547.4 jit_solution(7476831716049572928)
XLA Ops:
  0.0 4.2 subtract_bitcast_fusion.1
  6.8 8.8 %all-to-all-start = ((f32[4,16,64,256]{3,2,0,1:T(8,128)}), f32[4,16,64,256]{3,2,0,1:T(8,128)}, u32[]{:S(2)}, u32[]{:S(2)}) async-start(f32[4,16,64,256]{3,2,0,1:T(8,128)} %pad_maximum_fusion.4), calls=%async_computation | async-start | bytes 8388608 | tf_op jit(solution)/shard_map/all_to_all | solution.py:91
  17.3 64.8 %all-reduce.2 = (s32[1024]{0:T(1024)S(1)}, s32[1024]{0:T(1024)S(1)}) all-reduce(s32[1024]{0:T(1024)S(1)} %dynamic-update-slice, s32[1024]{0:T(1024)S(1)} %dynamic-update-slice.1), channel_id=1, replica_groups=mesh['ax'=8,'az'=16] {'az'}, use_global_device_ids=true, to_apply=%add | all-reduce | flops 2048 | bytes 16384
  84.6 23.9 %fusion.25 = f32[1024,2,256]{0,2,1:T(8,128)S(1)} fusion(s32[1024]{0:T(1024)S(1)} %get-tuple-element.56, f32[4,1,1024,256]{3,2,0,1:T(8,128)S(1)} %bitcast.190), kind=kOutput, calls=%fused_computation.52 | convolution fusion | flops 6458179584 | bytes 4198400 | tf_op jit(solution)/shard_map/prsx,sj->prjx/dot_general | solution.py:32
  108.5 23.5 %fusion.23 = f32[1024,2,256]{0,2,1:T(8,128)S(1)} fusion(s32[1024]{0:T(1024)S(1)} %get-tuple-element.56, f32[4,1,1024,256]{3,2,0,1:T(8,128)S(1)} %bitcast.191), kind=kOutput, calls=%fused_computation.50 | convolution fusion | flops 6458179584 | bytes 4198400 | tf_op jit(solution)/shard_map/prsx,sj->prjx/dot_general | solution.py:32
  132.1 23.6 %fusion.85 = f32[1024,2,256]{0,2,1:T(8,128)S(1)} fusion(f32[1024,2,256]{0,2,1:T(8,128)S(1)} %fusion.25, f32[4,1,1024,256]{3,2,0,1:T(8,128)S(1)} %bitcast.192, s32[1024]{0:T(1024)S(1)} %get-tuple-element.56), kind=kOutput, calls=%fused_computation.97 | convolution fusion | flops 6458703872 | bytes 6295552 | tf_op jit(solution)/shard_map/prsx,sj->prjx/dot_general | solution.py:32
  155.7 23.9 %add_bitcast_fusion = f32[2,1,1024,256]{2,3,1,0:T(8,128)S(1)} fusion(f32[1024,2,256]{0,2,1:T(8,128)S(1)} %fusion.23, f32[4,1,1024,256]{3,2,0,1:T(8,128)S(1)} %bitcast.193, s32[1024]{0:T(1024)S(1)} %get-tuple-element.56), kind=kOutput, calls=%fused_computation.77 | convolution fusion | flops 6458703872 | bytes 6295552 | tf_op jit(solution)/shard_map/prsx,sj->prjx/dot_general | solution.py:32
  182.8 5.1 collective-permute-start.1
  187.9 3.0 collective-permute-start.2
  190.9 30.7 %fusion.21 = f32[1024,4,256]{0,2,1:T(8,128)S(1)} fusion(s32[1024]{0:T(1024)S(1)} %get-tuple-element.56, f32[4,1024,256]{1,2,0:T(8,128)S(1)} %fusion.174), kind=kOutput, calls=%fused_computation.48 | convolution fusion | flops 12900630528 | bytes 8392704 | tf_op jit(solution)/shard_map/crjx,sj->crsx/dot_general | solution.py:32
  221.6 30.7 %fusion.27 = f32[1024,4,256]{0,2,1:T(8,128)S(1)} fusion(s32[1024]{0:T(1024)S(1)} %get-tuple-element.56, f32[4,1024,256]{1,2,0:T(8,128)S(1)} %fusion.176), kind=kOutput, calls=%fused_computation.54 | convolution fusion | flops 12900630528 | bytes 8392704 | tf_op jit(solution)/shard_map/crjx,sj->crsx/dot_general | solution.py:32
  253.4 30.4 %fusion.73 = f32[1024,4,256]{0,2,1:T(8,128)S(1)} fusion(f32[1024,4,256]{0,2,1:T(8,128)S(1)} %fusion.21, s32[1024]{0:T(1024)S(1)} %get-tuple-element.56, f32[4,1024,256]{1,2,0:T(8,128)S(1)} %fusion.178), kind=kOutput, calls=%fused_computation.91 | convolution fusion | flops 12901679104 | bytes 12587008 | tf_op jit(solution)/shard_map/crjx,sj->crsx/dot_general | solution.py:32
  284.8 30.8 %fusion.76 = f32[1024,4,256]{0,2,1:T(8,128)S(1)} fusion(f32[1024,4,256]{0,2,1:T(8,128)S(1)} %fusion.27, s32[1024]{0:T(1024)S(1)} %get-tuple-element.56, f32[4,1024,256]{1,2,0:T(8,128)S(1)} %fusion.180), kind=kOutput, calls=%fused_computation.92 | convolution fusion | flops 12901679104 | bytes 12587008 | tf_op jit(solution)/shard_map/crjx,sj->crsx/dot_general | solution.py:32
  322.4 4.4 pad_maximum_fusion.1
  326.8 10.2 %copy.91 = f32[4,2,1,1024,256]{4,0,2,1,3:T(4,128)} copy(f32[4,2,1,1024,256]{3,4,0,2,1:T(8,128)} %pad_maximum_fusion.1) | data formatting | bytes 16777216 | tf_op jit(solution)/shard_map/stack | solution.py:65
  337.1 6.7 %all-to-all-start.1 = ((f32[4,2,1,1024,256]{4,0,2,1,3:T(4,128)}), f32[4,2,1,1024,256]{4,0,2,1,3:T(4,128)}, u32[]{:S(2)}, u32[]{:S(2)}) async-start(f32[4,2,1,1024,256]{4,0,2,1,3:T(4,128)} %copy.91), calls=%async_computation.1 | async-start | bytes 16777216 | tf_op jit(solution)/shard_map/all_to_all | solution.py:116
  345.1 127.6 %all-to-all-done.1 = f32[4,2,1,1024,256]{4,0,2,1,3:T(4,128)} async-done(((f32[4,2,1,1024,256]{4,0,2,1,3:T(4,128)}), f32[4,2,1,1024,256]{4,0,2,1,3:T(4,128)}, u32[]{:S(2)}, u32[]{:S(2)}) %all-to-all-start.1) | async-done | bytes 8388640 | tf_op jit(solution)/shard_map/all_to_all | solution.py:116
  472.7 6.1 %copy.92 = f32[4,2,1,1024,256]{4,3,1,0,2:T(8,128)S(1)} copy(f32[4,2,1,1024,256]{4,0,2,1,3:T(4,128)} %all-to-all-done.1) | data formatting | bytes 16777216 | tf_op jit(solution)/shard_map/all_to_all | solution.py:116
  478.8 11.8 %fusion.43 = f32[4,2,16,64,256]{4,3,1,0,2:T(8,128)S(1)} fusion(f32[16,256]{1,0:T(8,128)S(1)} %copy_bitcast_fusion, f32[16,256]{1,0:T(8,128)S(1)} %get-tuple-element.76, pred[256,256]{1,0:T(8,128)(4,1)S(1)} %iota_compare_fusion, f32[4,2,16,64,256]{4,3,2,1,0:T(8,128)} %param.7, f32[4,2,16,64,256]{4,3,2,1,0:T(8,128)S(1)} %bitcast.189, ...), kind=kOutput, calls=%fused_computation.72 | convolution fusion | flops 6455033856 | bytes 25268224 | tf_op jit(solution)/shard_map/cdrmj,rji->cdrmi/dot_general | solution.py:32
  490.6 3.4 copy-done
  493.9 3.1 slice.124
  497.0 3.0 copy.94
  500.0 39.0 %while.10 = (s32[]{:T(128)}, f32[4,2,16,64]{3,2,1,0:T(8,128)S(1)}, pred[]{:T(512)}, f32[1,1,16,1]{2,3,1,0:T(1,128)S(1)}, f32[4,2,16,64]{3,2,1,0:T(8,128)S(1)}, /*index=5*/f32[4,2,16,64]{3,2,1,0:T(8,128)S(1)}, s32[]{:T(128)}) while((s32[]{:T(128)}, f32[4,2,16,64]{3,2,1,0:T(8,128)S(1)}, pred[]{:T(512)}, f32[1,1,16,1]{2,3,1,0:T(1,128)S(1)}, ...), condition=%wide.region_3.4_spmd, body=%wide.region_2.3_spmd.sunk | while | flops 24578 | bytes 327862 | solution.py:143
  500.1 3.5 collective-permute-start
  505.0 4.3 collective-permute-start
  510.7 4.3 collective-permute-start
  516.4 4.3 collective-permute-start
  522.1 4.3 collective-permute-start
  527.7 4.3 collective-permute-start
  533.4 4.3 collective-permute-start
  539.1 4.1 multiply_add_fusion.1
  543.2 4.0 copy.96
  (71 shorter events, 29.1 us)
Async XLA Ops:
  6.8 8.8 %copy-start.5 = (u32[128]{0:T(128)S(1)}, u32[128]{0:T(128)}, u32[]{:S(2)}) copy-start(u32[128]{0:T(128)} %constant.84) | copy-start | bytes 1540
  6.8 10.0 %copy-start.4 = (s32[64]{0:T(128)S(1)}, s32[64]{0:T(128)}, u32[]{:S(2)}) copy-start(s32[64]{0:T(128)} %param.10) | copy-start | bytes 772
  6.8 10.3 %copy-start.3 = (s32[64]{0:T(128)S(1)}, s32[64]{0:T(128)}, u32[]{:S(2)}) copy-start(s32[64]{0:T(128)} %param.11) | copy-start | bytes 772
  6.8 75.4 %all-to-all-start = ((f32[4,16,64,256]{3,2,0,1:T(8,128)}), f32[4,16,64,256]{3,2,0,1:T(8,128)}, u32[]{:S(2)}, u32[]{:S(2)}) async-start(f32[4,16,64,256]{3,2,0,1:T(8,128)} %pad_maximum_fusion.4), calls=%async_computation | async-start | bytes 8388608 | tf_op jit(solution)/shard_map/all_to_all | solution.py:91
  182.8 69.6 %collective-permute-start.1 = (f32[4,1,1024,1]{2,3,1,0:T(1,128)S(1)}, f32[4,1,1024,1]{2,3,1,0:T(1,128)S(1)}, u32[]{:S(2)}, u32[]{:S(2)}) collective-permute-start(f32[4,1,1024,1]{2,3,1,0:T(1,128)S(1)} %get-tuple-element.64), channel_id=1, source_target_pairs={{16,0},{32,16},{48,32},{64,48},{80,64},{96,80},{112,96},{17,1},{33... | collective-permute-start | bytes 49160 | tf_op jit(solution)/shard_map/ppermute | solution.py:20
  187.9 64.5 %collective-permute-start.2 = (f32[4,1,1024,1]{2,3,1,0:T(1,128)S(1)}, f32[4,1,1024,1]{2,3,1,0:T(1,128)S(1)}, u32[]{:S(2)}, u32[]{:S(2)}) collective-permute-start(f32[4,1,1024,1]{2,3,1,0:T(1,128)S(1)} %get-tuple-element.65), channel_id=1, source_target_pairs={{0,16},{16,32},{32,48},{48,64},{64,80},{80,96},{96,112},{1,17},{17... | collective-permute-start | bytes 49160 | tf_op jit(solution)/shard_map/ppermute | solution.py:17
  337.1 6.7 %copy-start.2 = (f32[16,256]{1,0:T(8,128)S(1)}, f32[16,256]{1,0:T(8,128)}, u32[]{:S(2)}) copy-start(f32[16,256]{1,0:T(8,128)} %param.9) | copy-start | bytes 49156
  337.1 8.0 %copy-start.1 = (f32[4,2,16,64]{3,2,1,0:T(8,128)S(1)}, f32[4,2,16,64]{3,2,1,0:T(8,128)}, u32[]{:S(2)}) copy-start(f32[4,2,16,64]{3,2,1,0:T(8,128)} %param.8) | copy-start | bytes 98308
  337.1 135.6 %all-to-all-start.1 = ((f32[4,2,1,1024,256]{4,0,2,1,3:T(4,128)}), f32[4,2,1,1024,256]{4,0,2,1,3:T(4,128)}, u32[]{:S(2)}, u32[]{:S(2)}) async-start(f32[4,2,1,1024,256]{4,0,2,1,3:T(4,128)} %copy.91), calls=%async_computation.1 | async-start | bytes 16777216 | tf_op jit(solution)/shard_map/all_to_all | solution.py:116
  490.5 3.4 copy-start
  500.1 4.8 collective-permute-start
  505.0 5.6 %collective-permute-start = (f32[4,2,16,64]{3,2,1,0:T(8,128)S(1)}, f32[4,2,16,64]{3,2,1,0:T(8,128)S(1)}, u32[]{:S(2)}, u32[]{:S(2)}) collective-permute-start(f32[4,2,16,64]{3,2,1,0:T(8,128)S(1)} %multiply_add_fusion.6), channel_id=1, source_target_pairs={{0,16},{16,32},{32,48},{48,64},{64,80},{80,96},{96,112},{1,17},{17... | collective-permute-start | bytes 98312 | tf_op jit(solution)/shard_map/while/body/eval_jaxpr/ppermute | solution.py:28
  510.7 5.6 %collective-permute-start = (f32[4,2,16,64]{3,2,1,0:T(8,128)S(1)}, f32[4,2,16,64]{3,2,1,0:T(8,128)S(1)}, u32[]{:S(2)}, u32[]{:S(2)}) collective-permute-start(f32[4,2,16,64]{3,2,1,0:T(8,128)S(1)} %multiply_add_fusion.6), channel_id=1, source_target_pairs={{0,16},{16,32},{32,48},{48,64},{64,80},{80,96},{96,112},{1,17},{17... | collective-permute-start | bytes 98312 | tf_op jit(solution)/shard_map/while/body/eval_jaxpr/ppermute | solution.py:28
  516.4 5.6 %collective-permute-start = (f32[4,2,16,64]{3,2,1,0:T(8,128)S(1)}, f32[4,2,16,64]{3,2,1,0:T(8,128)S(1)}, u32[]{:S(2)}, u32[]{:S(2)}) collective-permute-start(f32[4,2,16,64]{3,2,1,0:T(8,128)S(1)} %multiply_add_fusion.6), channel_id=1, source_target_pairs={{0,16},{16,32},{32,48},{48,64},{64,80},{80,96},{96,112},{1,17},{17... | collective-permute-start | bytes 98312 | tf_op jit(solution)/shard_map/while/body/eval_jaxpr/ppermute | solution.py:28
  522.1 5.6 %collective-permute-start = (f32[4,2,16,64]{3,2,1,0:T(8,128)S(1)}, f32[4,2,16,64]{3,2,1,0:T(8,128)S(1)}, u32[]{:S(2)}, u32[]{:S(2)}) collective-permute-start(f32[4,2,16,64]{3,2,1,0:T(8,128)S(1)} %multiply_add_fusion.6), channel_id=1, source_target_pairs={{0,16},{16,32},{32,48},{48,64},{64,80},{80,96},{96,112},{1,17},{17... | collective-permute-start | bytes 98312 | tf_op jit(solution)/shard_map/while/body/eval_jaxpr/ppermute | solution.py:28
  527.7 5.6 %collective-permute-start = (f32[4,2,16,64]{3,2,1,0:T(8,128)S(1)}, f32[4,2,16,64]{3,2,1,0:T(8,128)S(1)}, u32[]{:S(2)}, u32[]{:S(2)}) collective-permute-start(f32[4,2,16,64]{3,2,1,0:T(8,128)S(1)} %multiply_add_fusion.6), channel_id=1, source_target_pairs={{0,16},{16,32},{32,48},{48,64},{64,80},{80,96},{96,112},{1,17},{17... | collective-permute-start | bytes 98312 | tf_op jit(solution)/shard_map/while/body/eval_jaxpr/ppermute | solution.py:28
  533.4 5.6 %collective-permute-start = (f32[4,2,16,64]{3,2,1,0:T(8,128)S(1)}, f32[4,2,16,64]{3,2,1,0:T(8,128)S(1)}, u32[]{:S(2)}, u32[]{:S(2)}) collective-permute-start(f32[4,2,16,64]{3,2,1,0:T(8,128)S(1)} %multiply_add_fusion.6), channel_id=1, source_target_pairs={{0,16},{16,32},{32,48},{48,64},{64,80},{80,96},{96,112},{1,17},{17... | collective-permute-start | bytes 98312 | tf_op jit(solution)/shard_map/while/body/eval_jaxpr/ppermute | solution.py:28
where the time goes:
time: 551 us; the launch traced here: 547 us
  matrix products  229 us (42%)
  waiting for transfers between devices  137 us (25%)
  blocking collectives  64.8 us (12%)
  starting transfers between devices  52.6 us (10%)
  local copies, waits for them, and re-layouts  34.6 us (6%)
  other arithmetic  27.9 us (5%)
    dot_general x9, matrix products, contract(): jnp.einsum(pattern, operand_a, operand_b, precision=lax.Precision.HIGHEST)  229 us
    all_to_all x1, waiting for transfers between devices, shards(): lax.all_to_all(local_terms, 'az', split_axis=3, concat_axis=2, tiled=True)  128 us
    unnamed x1, blocking collectives  64.8 us
    ppermute x7, starting transfers between devices, from_behind(): return lax.ppermute(block, axis, route)  29 us
  transfers between devices with their start and end apart: 11, of which 8 were waited for; matrix products, arithmetic and copies ran while one was open for 12% of the time, Pallas kernels for 0%

commit v1 on v0

v1 whole, which is shorter than its diff:
```python
import functools
import math

import jax
import jax.numpy as jnp
from jax import lax
from jax.experimental import pallas as pl
from jax.experimental.pallas import tpu as pltpu
from jax.sharding import PartitionSpec as P

section_factor = 0.5
viscosity = 0.02
M = 1024
HALF = M // 2
FIELDS = 4
NR = 16
SLOTS = 64
CELLS = 256
NAZ = 16
NAX = 8
LANES = 128
MESH = pl.DeviceIdType.MESH
F32 = jnp.float32
BF16 = jnp.bfloat16


def split(value):
    high = value.astype(BF16)
    low = (value - high.astype(F32)).astype(BF16)
    return high, low


def inverse_radius(radial_id):
    ratio = (0.6 + 0.4 * (radial_id.astype(F32) + 0.5) / NR) * (M / (2.0 * math.pi))
    return 1.0 / ratio


def cos_sin(phase):
    quadrant = lax.shift_right_logical(phase + 128, 8)
    angle = (phase - quadrant * 256).astype(F32) * (2.0 * math.pi / M)
    square = angle * angle
    sine = angle * (
        1.0
        + square
        * (-1.0 / 6 + square * (1.0 / 120 + square * (-1.0 / 5040 + square * (1.0 / 362880))))
    )
    cosine = 1.0 + square * (
        -0.5 + square * (1.0 / 24 + square * (-1.0 / 720 + square * (1.0 / 40320)))
    )
    odd = (quadrant & 1) == 1
    norm = 1.0 / math.sqrt(M)
    cos_value = jnp.where(odd, sine, cosine)
    sin_value = jnp.where(odd, cosine, sine)
    cos_sign = jnp.where(((quadrant + 1) & 2) == 2, -norm, norm)
    sin_sign = jnp.where((quadrant & 2) == 2, -norm, norm)
    return cos_value * cos_sign, sin_value * sin_sign


def signed(modes):
    return jnp.where(modes < HALF, modes, jnp.where(modes == HALF, 0.0, modes - M))


def is_self(modes):
    return jnp.where((modes == 0.0) | (modes == float(HALF)), 1.0, 0.0)


def fold_rows(value):
    rows, lanes = value.shape
    return jnp.sum(value.reshape(rows // 8, 8, lanes), axis=0)


def kernel(
    state_ref, courant_ref, mode_ref, inflow_ref,
    acc_ref, incoming_ref, reach_ref,
    st, send_buf, x_buf, mode_buf, mode_sub, own_sub,
    cos_f, sin_f, cos_r, sin_r, rhs_a, rhs_b, tcat,
    fp, fm, fmid, d_mid, halo_send, halo_recv,
    lc_ref, lc_t, om_t, e_raw, e_send, e_recv, lhs_cat, rel_buf,
    st_sem, f_send, f_recv, m_send, m_recv, own_x, h_send, h_recv,
    e_send_sem, e_recv_sem, own_e, out_sem, rel_send, rel_recv,
):
    ax = lax.axis_index("ax")
    az = lax.axis_index("az")
    z = lax.div(az, 4)
    y = lax.rem(az, 4)

    def az_target(offset):
        return lax.rem(z + lax.div(offset, 4), 4) * 4 + lax.rem(y + lax.rem(offset, 4), 4)

    def ax_target(offset):
        return lax.rem(ax + offset, NAX)

    def start_state(offset, carry):
        target = az_target(offset)
        pltpu.make_async_copy(
            state_ref.at[:, :, target], st.at[target], st_sem.at[target]
        ).start()
        return carry

    lax.fori_loop(0, NAZ, start_state, 0)

    barrier = pltpu.get_barrier_semaphore()

    def greet_az(offset, carry):
        pl.semaphore_signal(barrier, inc=1, device_id=(ax, az_target(offset)), device_id_type=MESH)
        return carry

    def greet_ax(offset, carry):
        pl.semaphore_signal(barrier, inc=1, device_id=(ax_target(offset), az), device_id_type=MESH)
        return carry

    lax.fori_loop(1, NAZ, greet_az, 0)
    lax.fori_loop(1, NAX, greet_ax, 0)

    mode_buf[az] = mode_ref[...]
    pl.semaphore_wait(barrier, NAZ - 1 + NAX - 1)

    def send_modes(offset, carry):
        pltpu.make_async_remote_copy(
            src_ref=mode_ref, dst_ref=mode_buf.at[az], send_sem=m_send, recv_sem=m_recv,
            device_id=(ax, az_target(offset)), device_id_type=MESH,
        ).start()
        return carry

    lax.fori_loop(1, NAZ, send_modes, 0)

    def send_piece(target, chunk, pair):
        comps = pl.ds(pair * 2, 2)
        pltpu.make_async_remote_copy(
            src_ref=send_buf.at[target, chunk, comps],
            dst_ref=x_buf.at[chunk, comps, pl.ds(az * SLOTS, SLOTS), :],
            send_sem=f_send, recv_sem=f_recv.at[chunk],
            device_id=(ax, target), device_id_type=MESH,
        ).start()

    def pack(offset, carry):
        target = az_target(offset)
        pltpu.make_async_copy(
            state_ref.at[:, :, target], st.at[target], st_sem.at[target]
        ).wait()
        for pair in range(2):
            for chunk in range(2):
                cells = pl.ds(chunk * LANES, LANES)
                send_buf[target, chunk, 2 * pair] = (
                    st[target, 2 * pair, 0, :, cells] - st[target, 2 * pair + 1, 1, :, cells]
                )
                send_buf[target, chunk, 2 * pair + 1] = (
                    st[target, 2 * pair, 1, :, cells] + st[target, 2 * pair + 1, 0, :, cells]
                )

        @pl.when(offset > 0)
        def _():
            send_piece(target, 0, 0)

        return carry

    lax.fori_loop(0, NAZ, pack, 0)
    for chunk, pair in ((0, 1), (1, 0), (1, 1)):

        def send_more(offset, carry, chunk=chunk, pair=pair):
            send_piece(az_target(offset), chunk, pair)
            return carry

        lax.fori_loop(1, NAZ, send_more, 0)

    def own_copy(chunk):
        return pltpu.make_async_copy(
            send_buf.at[az, chunk],
            x_buf.at[chunk, :, pl.ds(az * SLOTS, SLOTS), :],
            own_x.at[chunk],
        )

    own_copy(0).start()
    own_copy(1).start()

    courant = courant_ref[...]
    log_weight = -jnp.log(1.0 + 1.0 / courant)
    row_ids = lax.broadcasted_iota(jnp.int32, (CELLS, CELLS), 0)
    col_ids = lax.broadcasted_iota(jnp.int32, (CELLS, CELLS), 1)
    upper = jnp.where(row_ids <= col_ids, 1.0, 0.0)
    log_cum = jnp.dot(
        log_weight, upper, preferred_element_type=F32, precision=lax.Precision.HIGHEST
    )
    lc_ref[...] = log_cum
    reach_ref[...] = jnp.exp(log_cum)
    lc_t[...] = jnp.concatenate([log_cum] * 8, axis=0).T
    om_t[...] = jnp.concatenate([1.0 / (1.0 + courant)] * 8, axis=0).T

    def build_transfer(radial, scale):
        row = lc_ref[pl.ds(radial, 1), :]
        lanes = lax.broadcasted_iota(jnp.int32, (SLOTS, LANES), 1)

        def body(block, carry):
            rows = pl.ds(pl.multiple_of(block * SLOTS, SLOTS), SLOTS)
            pick = lanes == radial
            lc_col = jnp.sum(jnp.where(pick, lc_t[rows, :], 0.0), axis=1, keepdims=True)
            om_col = jnp.sum(jnp.where(pick, om_t[rows, :], 0.0), axis=1, keepdims=True)
            source = block * SLOTS + lax.broadcasted_iota(jnp.int32, (SLOTS, CELLS), 0)
            cell = lax.broadcasted_iota(jnp.int32, (SLOTS, CELLS), 1)
            value = jnp.where(
                source <= cell, (om_col * scale) * jnp.exp(jnp.minimum(row - lc_col, 0.0)), 0.0
            )
            high, low = split(value)
            tcat[rows, :] = high
            tcat[pl.ds(pl.multiple_of(CELLS + block * SLOTS, SLOTS), SLOTS), :] = low
            tcat[pl.ds(pl.multiple_of(2 * CELLS + block * SLOTS, SLOTS), SLOTS), :] = high
            return carry

        lax.fori_loop(0, CELLS // SLOTS, body, 0)

    build_transfer(az, section_factor)

    pltpu.make_async_copy(mode_buf.at[pl.ds(0, NAZ - 1)], mode_buf.at[pl.ds(0, NAZ - 1)], m_recv).wait()
    first_lanes = lax.broadcasted_iota(jnp.int32, (8, LANES), 1) < SLOTS
    mode_lane = [
        jnp.where(first_lanes, mode_buf[2 * q], mode_buf[2 * q + 1]) for q in range(4)
    ]
    for q in range(4):
        wide = jnp.concatenate([mode_lane[q].astype(F32)] * 16, axis=0)
        mode_sub[pl.ds(q * LANES, LANES), :] = wide.T
    own_sub[...] = jnp.concatenate([mode_buf[az].astype(F32)] * 16, axis=0).T[:SLOTS, :]
    mode_row = jnp.concatenate(mode_lane, axis=1)[0:1, :]

    def tables(block, carry):
        rows = pl.ds(pl.multiple_of(block * 16, 16), 16)
        point = block * 16 + lax.broadcasted_iota(jnp.int32, (16, HALF), 0)
        cos_value, sin_value = cos_sin((mode_row * point) & (M - 1))
        for table, value in ((cos_f, cos_value), (sin_f, sin_value)):
            high, low = split(value)
            table[rows, 0:HALF] = high
            table[rows, HALF : 2 * HALF] = high
            table[rows, 2 * HALF : 3 * HALF] = low
        mode_col = mode_sub[rows, :].astype(jnp.int32)
        for q in range(4):
            lane_point = q * LANES + lax.broadcasted_iota(jnp.int32, (16, LANES), 1)
            cos_value, sin_value = cos_sin((mode_col * lane_point) & (M - 1))
            cos_value = jnp.where(lane_point == 0, 0.5 * cos_value, cos_value)
            for table, value in ((cos_r, cos_value), (sin_r, sin_value)):
                high, low = split(value)
                table[rows, q * LANES : (q + 1) * LANES] = high
                table[rows, HALF + q * LANES : HALF + (q + 1) * LANES] = high
                table[rows, 2 * HALF + q * LANES : 2 * HALF + (q + 1) * LANES] = low
        return carry

    lax.fori_loop(0, HALF // 16, tables, 0)

    def self_mode(block, carry):
        modes = mode_sub[pl.ds(pl.multiple_of(block * 8, 8), 8), :]
        return carry + modes * is_self(modes)

    first_self = jnp.sum(
        lax.fori_loop(0, HALF // 8, self_mode, jnp.zeros((8, LANES), F32)), axis=0, keepdims=True
    )
    second_is_half = first_self == 0.0
    norm = 1.0 / math.sqrt(M)

    def second_cos(rows, start):
        point = start + lax.broadcasted_iota(jnp.int32, (rows, LANES), 0)
        return jnp.where(second_is_half & ((point & 1) == 1), -norm, norm)

    def put_rhs(buf, block, lanes, value):
        high, low = split(value)
        start = block * SLOTS
        buf[pl.ds(pl.multiple_of(start, SLOTS), SLOTS), lanes] = high
        buf[pl.ds(pl.multiple_of(HALF + start, SLOTS), SLOTS), lanes] = low
        buf[pl.ds(pl.multiple_of(2 * HALF + start, SLOTS), SLOTS), lanes] = high

    def forward(chunk, carry):
        own_copy(chunk).wait()
        arrived = x_buf.at[chunk, :, pl.ds(0, (NAZ - 1) * SLOTS), :]
        pltpu.make_async_copy(arrived, arrived, f_recv.at[chunk]).wait()

        def fold(block, sums):
            modes = mode_sub[pl.ds(pl.multiple_of(block * SLOTS, SLOTS), SLOTS), :]
            alone = is_self(modes)
            parity = jnp.where((modes.astype(jnp.int32) & 1) == 1, -norm, norm)
            out = []
            for comp in range(4):
                one = x_buf[chunk, comp, pl.ds(pl.multiple_of(block * SLOTS, SLOTS), SLOTS), :]
                two = x_buf[chunk, comp, pl.ds(pl.multiple_of(HALF + block * SLOTS, SLOTS), SLOTS), :]
                even = one + (1.0 - alone) * two
                odd = (one - two) if comp % 2 == 1 else (two - one)
                put_rhs(rhs_a, block, pl.ds(comp * LANES, LANES), even)
                put_rhs(rhs_b, block, pl.ds((comp ^ 1) * LANES, LANES), odd)
                out.append(sums[comp] + fold_rows(alone * two))
                out.append(sums[4 + comp] + fold_rows(parity * even))
            return tuple(out[0::2] + out[1::2])

        zero = jnp.zeros((8, LANES), F32)
        sums = lax.fori_loop(0, HALF // SLOTS, fold, (zero,) * 8)
        alone_rows = [jnp.sum(sums[c], axis=0, keepdims=True) for c in range(4)]
        for c in range(4):
            middle = jnp.sum(sums[4 + c], axis=0, keepdims=True) + alone_rows[c] * norm
            fmid[chunk, c] = jnp.broadcast_to(middle, (8, LANES))
        for pair in range(2):
            lanes = slice(pair * 2 * LANES, (pair + 1) * 2 * LANES)
            fp[chunk, 2 * pair : 2 * pair + 2] = jnp.stack(
                jnp.split(
                    jnp.dot(cos_f[...], rhs_a[:, lanes], preferred_element_type=F32), 2, axis=1
                )
            )
            fm[chunk, 2 * pair : 2 * pair + 2] = jnp.stack(
                jnp.split(
                    jnp.dot(sin_f[...], rhs_b[:, lanes], preferred_element_type=F32), 2, axis=1
                )
            )

        def combine(block, carry):
            rows = pl.ds(pl.multiple_of(block * SLOTS, SLOTS), SLOTS)
            second = second_cos(SLOTS, block * SLOTS)
            for c in range(4):
                even = fp[chunk, c, rows, :] + second * alone_rows[c]
                odd = fm[chunk, c, rows, :]
                fp[chunk, c, rows, :] = even - odd
                fm[chunk, c, rows, :] = even + odd
            return carry

        lax.fori_loop(0, HALF // SLOTS, combine, 0)
        return carry

    lax.fori_loop(0, 2, forward, 0)

    lane64 = lax.broadcasted_iota(jnp.int32, (SLOTS, LANES), 1)
    lane8 = lax.broadcasted_iota(jnp.int32, (8, LANES), 1)

    def edges(block, carry):
        rows = pl.ds(pl.multiple_of(block * SLOTS, SLOTS), SLOTS)
        for side, chunk, lane in ((0, 1, LANES - 1), (1, 0, 0)):
            tile = jnp.zeros((SLOTS, LANES), F32)
            for c in range(4):
                tile = jnp.where(lane64 == c, fp[chunk, c, rows, lane : lane + 1], tile)
                tile = jnp.where(lane64 == 4 + c, fm[chunk, c, rows, lane : lane + 1], tile)
            halo_send[side, rows, :] = tile
        return carry

    lax.fori_loop(0, HALF // SLOTS, edges, 0)
    for side, chunk, lane in ((0, 1, LANES - 1), (1, 0, 0)):
        tile = jnp.zeros((8, LANES), F32)
        for c in range(4):
            tile = jnp.where(lane8 == c, fmid[chunk, c, :, lane : lane + 1], tile)
        halo_send[side, pl.ds(HALF, 8), :] = tile

    def halo_copy(side):
        return pltpu.make_async_remote_copy(
            src_ref=halo_send.at[side], dst_ref=halo_recv.at[side],
            send_sem=h_send.at[side], recv_sem=h_recv.at[side],
            device_id=(ax_target(1 if side == 0 else NAX - 1), az), device_id_type=MESH,
        )

    halo_copy(0).start()
    halo_copy(1).start()
    halo_copy(0).wait()
    halo_copy(1).wait()
    left_on = jnp.where(ax > 0, 1.0, 0.0)
    right_on = jnp.where(ax < NAX - 1, 1.0, 0.0)
    here = inverse_radius(az)
    here_square = here * here

    def flux_pair(get, rows, c, left_lane0, left_lanec, cell):
        first = jnp.concatenate([get(0, 0), get(1, 0)], axis=1)
        this = jnp.concatenate([get(0, c), get(1, c)], axis=1)
        third = jnp.concatenate([get(0, 2), get(1, 2)], axis=1)
        axial = first * this
        after = pltpu.roll(axial, CELLS - 1, axis=1)
        before = pltpu.roll(axial, 1, axis=1)
        left, right = left_lane0, left_lanec
        before = jnp.where(cell == 0, left, before)
        after = jnp.where(cell == CELLS - 1, right, after)
        return (before - after) * 0.5, third * this

    def pick_lane(tile, lanes, index):
        return jnp.sum(jnp.where(lanes == index, tile, 0.0), axis=1, keepdims=True)

    def explicit(c, carry):
        def fluxes(block, sums):
            rows = pl.ds(pl.multiple_of(block * SLOTS, SLOTS), SLOTS)
            cell = lax.broadcasted_iota(jnp.int32, (SLOTS, CELLS), 1)
            tile_l = halo_recv[0, rows, :]
            tile_r = halo_recv[1, rows, :]
            both = []
            for shift, source in ((0, fp), (4, fm)):
                left = tile_l[:, shift : shift + 1] * pick_lane(tile_l, lane64, c + shift) * left_on
                right = tile_r[:, shift : shift + 1] * pick_lane(tile_r, lane64, c + shift) * right_on
                both.append(
                    flux_pair(
                        lambda chunk, field, source=source: source[chunk, field, rows, :],
                        rows, c, left, right, cell,
                    )
                )
            (div_p, azi_p), (div_m, azi_m) = both
            div_even = div_p + div_m
            put_rhs(rhs_a, block, pl.ds(0, CELLS), div_even)
            put_rhs(rhs_a, block, pl.ds(CELLS, CELLS), azi_p + azi_m)
            put_rhs(rhs_b, block, pl.ds(0, CELLS), div_p - div_m)
            put_rhs(rhs_b, block, pl.ds(CELLS, CELLS), azi_p - azi_m)
            second = second_cos(SLOTS, block * SLOTS)
            point = block * SLOTS + lax.broadcasted_iota(jnp.int32, (SLOTS, LANES), 0)
            second = jnp.where(point == 0, 0.5 * second, second)
            second = jnp.concatenate([second, second], axis=1)
            return sums + fold_rows(second * div_even)

        second_sum = lax.fori_loop(0, HALF // SLOTS, fluxes, jnp.zeros((8, CELLS), F32))
        tile_l = halo_recv[0, pl.ds(HALF, 8), :]
        tile_r = halo_recv[1, pl.ds(HALF, 8), :]
        cell = lax.broadcasted_iota(jnp.int32, (8, CELLS), 1)
        div_mid, azi_mid = flux_pair(
            lambda chunk, field: fmid[chunk, field], None, c,
            tile_l[:, 0:1] * pick_lane(tile_l, lane8, c) * left_on,
            tile_r[:, 0:1] * pick_lane(tile_r, lane8, c) * right_on,
            cell,
        )
        div_mid = div_mid[0:1, :]
        azi_mid = azi_mid[0:1, :]
        second_row = jnp.sum(second_sum, axis=0, keepdims=True) + div_mid * norm

        for half in range(2):
            lanes = slice(half * CELLS, (half + 1) * CELLS)
            e_raw[half] = jnp.dot(cos_r[...], rhs_a[:, lanes], preferred_element_type=F32)
            e_raw[2 + half] = jnp.dot(sin_r[...], rhs_b[:, lanes], preferred_element_type=F32)

        def finish(block, carry):
            rows = pl.ds(pl.multiple_of(block * SLOTS, SLOTS), SLOTS)
            modes = mode_sub[rows, :]
            parity = jnp.where((modes.astype(jnp.int32) & 1) == 1, -norm, norm)
            wave = signed(modes) * here_square
            alone = is_self(modes)
            parity, wave, alone = (jnp.concatenate([v, v], axis=1) for v in (parity, wave, alone))
            cos_div = e_raw[0, rows, :] + parity * div_mid
            cos_azi = e_raw[1, rows, :] + parity * azi_mid
            real = cos_div - wave * e_raw[3, rows, :]
            imag = alone * second_row - e_raw[2, rows, :] - wave * cos_azi
            for part, value in ((0, real), (1, imag)):
                high, low = split(value)
                where = pl.ds(pl.multiple_of(part * HALF + block * SLOTS, SLOTS), SLOTS)
                lhs_cat[where, 0:CELLS] = high
                lhs_cat[where, CELLS : 2 * CELLS] = high
                lhs_cat[where, 2 * CELLS : 3 * CELLS] = low
            return carry

        lax.fori_loop(0, HALF // SLOTS, finish, 0)
        for part in range(2):
            e_send[c, part] = jnp.dot(
                lhs_cat[part * HALF : (part + 1) * HALF, :], tcat[...], preferred_element_type=F32
            )
        pltpu.make_async_copy(
            e_send.at[c, :, pl.ds(lax.rem(az, 8) * SLOTS, SLOTS), :], e_recv.at[c, az], own_e.at[c]
        ).start()

        for part in range(2):

            def send_back(offset, carry, part=part):
                target = az_target(offset)
                pltpu.make_async_remote_copy(
                    src_ref=e_send.at[c, part, pl.ds(lax.rem(target, 8) * SLOTS, SLOTS), :],
                    dst_ref=e_recv.at[c, az, part],
                    send_sem=e_send_sem, recv_sem=e_recv_sem.at[c],
                    device_id=(ax, target), device_id_type=MESH,
                ).start()
                return carry

            lax.fori_loop(1, NAZ, send_back, 0)
        return carry

    lax.fori_loop(0, FIELDS, explicit, 0)

    def state_sweep(radial, carry):
        build_transfer(radial, 1.0)
        there = inverse_radius(radial)
        ratio = signed(own_sub[...]) * there
        keep = 1.0 - (section_factor * viscosity) * ratio * ratio
        keep = jnp.concatenate([keep, keep], axis=1)
        for c in range(FIELDS):
            for part in range(2):
                high, low = split(st[radial, c, part] * keep)
                rows = pl.ds((2 * c + part) * SLOTS, SLOTS)
                lhs_cat[rows, 0:CELLS] = high
                lhs_cat[rows, CELLS : 2 * CELLS] = high
                lhs_cat[rows, 2 * CELLS : 3 * CELLS] = low
        swept = jnp.dot(lhs_cat[0:HALF, :], tcat[...], preferred_element_type=F32)
        st[radial] = swept.reshape(FIELDS, 2, SLOTS, CELLS)
        return carry

    lax.fori_loop(0, NR, state_sweep, 0)

    low_half = jnp.where(z < 2, 1.0, 0.0)
    own_alone = is_self(own_sub[...])
    swap = own_alone * (1.0 - low_half)
    flip = (1.0 - own_alone) * (2.0 * low_half - 1.0)
    swap = jnp.concatenate([swap, swap], axis=1)
    flip = jnp.concatenate([flip, flip], axis=1)

    def arrive(c, last):
        pltpu.make_async_copy(
            e_send.at[c, :, pl.ds(lax.rem(az, 8) * SLOTS, SLOTS), :], e_recv.at[c, az], own_e.at[c]
        ).wait()
        arrived = e_recv.at[c, pl.ds(0, NAZ - 1)]
        pltpu.make_async_copy(arrived, arrived, e_recv_sem.at[c]).wait()

        def add(radial, last):
            real = e_recv[c, radial, 0]
            imag = e_recv[c, radial, 1]
            new_real = st[radial, c, 0] + real + swap * (imag - real)
            new_imag = st[radial, c, 1] + flip * imag
            st[radial, c, 0] = new_real
            st[radial, c, 1] = new_imag
            where = c * 2 * NR + radial
            last = jnp.where(lane64 == where, new_real[:, CELLS - 1 : CELLS], last)
            last = jnp.where(lane64 == where + NR, new_imag[:, CELLS - 1 : CELLS], last)
            pltpu.make_async_copy(st.at[radial, c], acc_ref.at[c, :, radial], out_sem.at[c]).start()
            return last

        return lax.fori_loop(0, NR, add, last)

    last = lax.fori_loop(0, FIELDS, arrive, jnp.zeros((SLOTS, LANES), F32))

    rel_buf[ax, pl.ds(0, SLOTS), :] = last
    decay_row = jnp.exp(lc_t[pl.ds(CELLS - 8, 8), :])[7:8, :]
    rel_buf[ax, pl.ds(SLOTS, 8), :] = jnp.broadcast_to(decay_row, (8, LANES))

    def send_last(offset, carry):
        pltpu.make_async_remote_copy(
            src_ref=rel_buf.at[ax], dst_ref=rel_buf.at[ax], send_sem=rel_send, recv_sem=rel_recv,
            device_id=(ax_target(offset), az), device_id_type=MESH,
        ).start()
        return carry

    lax.fori_loop(1, NAX, send_last, 0)
    others = rel_buf.at[pl.ds(0, NAX - 1)]
    pltpu.make_async_copy(others, others, rel_recv).wait()

    def relay(block, incoming):
        upstream = rel_buf[block, pl.ds(0, SLOTS), :]
        decay = rel_buf[block, pl.ds(SLOTS, 8), :][0:1, :]
        return jnp.where(block < ax, decay * incoming + upstream, incoming)

    incoming_ref[...] = lax.fori_loop(0, NAX - 1, relay, inflow_ref[...])

    pltpu.make_async_copy(others, others, rel_send).wait()
    pltpu.make_async_copy(
        mode_buf.at[pl.ds(0, NAZ - 1)], mode_buf.at[pl.ds(0, NAZ - 1)], m_send
    ).wait()
    sent = send_buf.at[pl.ds(0, NAZ - 1)]
    pltpu.make_async_copy(sent, sent, f_send).wait()
    sent_back = e_recv.at[:, pl.ds(0, NAZ - 1)]
    pltpu.make_async_copy(sent_back, sent_back, e_send_sem).wait()

    def written(c, carry):
        pltpu.make_async_copy(acc_ref.at[c], acc_ref.at[c], out_sem.at[c]).wait()
        return carry

    lax.fori_loop(0, FIELDS, written, 0)


def shards(state, inflow, courant, mode_number, partner_table):
    modes = jnp.broadcast_to(jnp.concatenate([mode_number, mode_number])[None, :], (8, LANES))
    inflow_tile = inflow.reshape(FIELDS * 2 * NR, SLOTS).T
    dma = pltpu.SemaphoreType.DMA
    vmem = pltpu.VMEM
    acc, incoming, reach = pl.pallas_call(
        kernel,
        out_shape=(
            jax.ShapeDtypeStruct((FIELDS, 2, NR, SLOTS, CELLS), F32),
            jax.ShapeDtypeStruct((SLOTS, LANES), F32),
            jax.ShapeDtypeStruct((NR, CELLS), F32),
        ),
        in_specs=[
            pl.BlockSpec(memory_space=pl.ANY),
            pl.BlockSpec(memory_space=pltpu.VMEM),
            pl.BlockSpec(memory_space=pltpu.VMEM),
            pl.BlockSpec(memory_space=pltpu.VMEM),
        ],
        out_specs=(
            pl.BlockSpec(memory_space=pl.ANY),
            pl.BlockSpec(memory_space=pltpu.VMEM),
            pl.BlockSpec(memory_space=pltpu.VMEM),
        ),
        scratch_shapes=[
            vmem((NR, FIELDS, 2, SLOTS, CELLS), F32),
            vmem((NAZ, 2, 4, SLOTS, LANES), F32),
            vmem((2, 4, M, LANES), F32),
            vmem((NAZ, 8, LANES), jnp.int32),
            vmem((HALF, LANES), F32),
            vmem((SLOTS, LANES), F32),
            vmem((HALF, 3 * HALF), BF16),
            vmem((HALF, 3 * HALF), BF16),
            vmem((HALF, 3 * HALF), BF16),
            vmem((HALF, 3 * HALF), BF16),
            vmem((3 * HALF, 4 * LANES), BF16),
            vmem((3 * HALF, 4 * LANES), BF16),
            vmem((3 * CELLS, CELLS), BF16),
            vmem((2, FIELDS, HALF, LANES), F32),
            vmem((2, FIELDS, HALF, LANES), F32),
            vmem((2, FIELDS, 8, LANES), F32),
            vmem((8, LANES), F32),
            vmem((2, HALF + 8, LANES), F32),
            vmem((2, HALF + 8, LANES), F32),
            vmem((NR, CELLS), F32),
            vmem((CELLS, LANES), F32),
            vmem((CELLS, LANES), F32),
            vmem((4, HALF, CELLS), F32),
            vmem((FIELDS, 2, HALF, CELLS), F32),
            vmem((FIELDS, NAZ, 2, SLOTS, CELLS), F32),
            vmem((M, 3 * CELLS), BF16),
            vmem((NAX, SLOTS + 8, LANES), F32),
            dma((NAZ,)),
            dma,
            dma((2,)),
            dma,
            dma,
            dma((2,)),
            dma((2,)),
            dma((2,)),
            dma,
            dma((FIELDS,)),
            dma((FIELDS,)),
            dma((FIELDS,)),
            dma,
            dma,
        ],
        compiler_params=pltpu.CompilerParams(
            collective_id=0, has_side_effects=True, vmem_limit_bytes=58 * 2**20
        ),
    )(state, courant, modes, inflow_tile)
    incoming_full = incoming.T.reshape(FIELDS, 2, NR, SLOTS)
    return acc + reach[None, None, :, None, :] * incoming_full[..., None]


def solution(mesh):
    in_specs = (
        P(None, None, None, "az", "ax"),
        P(None, None, None, "az"),
        P(None, "ax"),
        P("az"),
        P("az"),
    )
    out_specs = P(None, None, None, "az", "ax")
    return jax.shard_map(shards, mesh=mesh, in_specs=in_specs, out_specs=out_specs, check_vma=False)
```

time: 551 us -> 196 us (0.36)
  matrix products: 229 us -> 0 us
  Pallas kernels: 0 us -> 183 us
  waiting for transfers between devices: 137 us -> 0 us
  blocking collectives: 64.8 us -> 0 us
  starting transfers between devices: 52.6 us -> 0 us
  local copies, waits for them, and re-layouts: 34.6 us -> 2.97 us
  other arithmetic: 27.9 us -> 7.01 us
    dot_general x9 -> x0, matrix products: 229 us -> none  [contract(): jnp.einsum(pattern, operand_a, operand_b, precision=lax.Precision.HIGHEST)]
    pallas_call x0 -> x1, Pallas kernels: none -> 183 us  [shards(): pl.pallas_call(kernel, out_shape=(jax.ShapeDtypeStruct((FIELDS, 2, NR, SL...]
    all_to_all x2 -> x0, waiting for transfers between devices: 128 us -> none  [the longest x1 128 us: shards(): lax.all_to_all(local_terms, 'az', split_axis=3, concat_axis=2, tiled=True)]
    unnamed x1 -> x0, blocking collectives: 64.8 us -> none
    ppermute x9 -> x0, starting transfers between devices: 37.1 us -> none  [the longest x7 29 us: from_behind(): return lax.ppermute(block, axis, route)]
    all_to_all x2 -> x0, starting transfers between devices: 15.5 us -> none  [the longest x1 8.78 us: shards(): lax.all_to_all(packed, 'az', split_axis=1, concat_axis=2, tiled=True)]
    another operation x8 -> x0, other arithmetic: 11.9 us -> none  [the longest x3 7.44 us: untangle(): return jnp.stack([real_terms, imag_terms], axis=1)]
    another operation x3 -> x0, local copies, waits for them, and re-layouts: 10.4 us -> none  [the longest x1 10.2 us: untangle(): return jnp.stack([real_terms, imag_terms], axis=1)]
  transfers between devices with their start and end apart: 11 -> 0, of which waited for: 8 -> 0; matrix products, arithmetic and copies ran while one was open for 12% -> 0% of each run, Pallas kernels for 0% -> 0%
where the time goes in v1:
time: 196 us; the launch traced here: 193 us
  Pallas kernels  183 us (93%)
  other arithmetic  7.01 us (4%)
  local copies, waits for them, and re-layouts  2.97 us (2%)
    pallas_call x1, Pallas kernels, shards(): pl.pallas_call(kernel, out_shape=(jax.ShapeDtypeStruct((FIELDS, 2, NR, SL...  183 us
    add x1, other arithmetic, shards(): return acc + reach[None, None, :, None, :] * incoming_full[..., None]  6.21 us

profile of v1, /device:TPU:1, one launch (start us, length us, event | category | flops | bytes accessed | tf_op | source)
XLA Modules:
  0.0 193.4 jit_solution(11564732342082953828)
XLA Ops:
  0.0 0.8 pad_add_fusion
  0.8 0.6 broadcast_in_dim.2.mode_ref
  1.4 1.5 copy.7
  2.9 183.3 %shard_map.46 = (f32[4,2,16,64,256]{4,3,2,1,0:T(8,128)}, f32[64,128]{1,0:T(8,128)}, f32[16,256]{1,0:T(8,128)}) custom-call(f32[4,2,16,64,256]{4,3,2,1,0:T(8,128)} %state_ref.1, f32[16,256]{1,0:T(8,128)} %courant_ref.1, s32[8,128]{1,0:T(8,128)} %broadcast_in_dim.2.mode_ref, f32[64,128]{1,0:T(8,128)} %bitcast.5), custom_call_target="tpu_custom_call" | custom-call | tf_op jit(solution)/shard_map/pallas_call | solution.py:559
  186.3 0.8 copy.8
  187.1 6.2 %multiply_add_fusion = f32[4,2,16,64,256]{4,3,2,1,0:T(8,128)} fusion(f32[4,2,16,64,256]{4,3,2,1,0:T(8,128)} %get-tuple-element.8, f32[4,2,16,64]{3,2,1,0:T(8,128)S(1)} %bitcast.4, f32[16,256]{1,0:T(8,128)} %get-tuple-element.9), kind=kLoop, calls=%fused_computation | loop fusion | flops 4194304 | bytes 16826368 | tf_op jit(solution)/shard_map/add | solution.py:625

commit v2 on v1

--- a/solution.py
+++ b/solution.py
@@ -74,7 +74,7 @@
     acc_ref, incoming_ref, reach_ref,
     st, send_buf, x_buf, mode_buf, mode_sub, own_sub,
     cos_f, sin_f, cos_r, sin_r, rhs_a, rhs_b, tcat,
-    fp, fm, fmid, d_mid, halo_send, halo_recv,
+    fp, fm, fmid, halo_send, halo_recv,
     lc_ref, lc_t, om_t, e_raw, e_send, e_recv, lhs_cat, rel_buf,
     st_sem, f_send, f_recv, m_send, m_recv, own_x, h_send, h_recv,
     e_send_sem, e_recv_sem, own_e, out_sem, rel_send, rel_recv,
@@ -85,7 +85,8 @@
     y = lax.rem(az, 4)
 
     def az_target(offset):
-        return lax.rem(z + lax.div(offset, 4), 4) * 4 + lax.rem(y + lax.rem(offset, 4), 4)
+        step = lax.rem(offset * 7, NAZ)
+        return lax.rem(z + lax.div(step, 4), 4) * 4 + lax.rem(y + lax.rem(step, 4), 4)
 
     def ax_target(offset):
         return lax.rem(ax + offset, NAX)
@@ -112,69 +113,86 @@
     lax.fori_loop(1, NAZ, greet_az, 0)
     lax.fori_loop(1, NAX, greet_ax, 0)
 
-    mode_buf[az] = mode_ref[...]
-    pl.semaphore_wait(barrier, NAZ - 1 + NAX - 1)
-
-    def send_modes(offset, carry):
-        pltpu.make_async_remote_copy(
-            src_ref=mode_ref, dst_ref=mode_buf.at[az], send_sem=m_send, recv_sem=m_recv,
-            device_id=(ax, az_target(offset)), device_id_type=MESH,
-        ).start()
-        return carry
-
-    lax.fori_loop(1, NAZ, send_modes, 0)
-
-    def send_piece(target, chunk, pair):
-        comps = pl.ds(pair * 2, 2)
-        pltpu.make_async_remote_copy(
-            src_ref=send_buf.at[target, chunk, comps],
-            dst_ref=x_buf.at[chunk, comps, pl.ds(az * SLOTS, SLOTS), :],
-            send_sem=f_send, recv_sem=f_recv.at[chunk],
-            device_id=(ax, target), device_id_type=MESH,
-        ).start()
+    modes_here = mode_ref[...]
+    mode_buf[az] = jnp.broadcast_to(jnp.concatenate([modes_here, modes_here], axis=1), (8, LANES))
 
     def pack(offset, carry):
         target = az_target(offset)
         pltpu.make_async_copy(
             state_ref.at[:, :, target], st.at[target], st_sem.at[target]
         ).wait()
+        low_lanes = lax.broadcasted_iota(jnp.int32, (SLOTS, LANES), 1) < LANES // 2
         for pair in range(2):
-            for chunk in range(2):
-                cells = pl.ds(chunk * LANES, LANES)
-                send_buf[target, chunk, 2 * pair] = (
-                    st[target, 2 * pair, 0, :, cells] - st[target, 2 * pair + 1, 1, :, cells]
+            one, two = 2 * pair, 2 * pair + 1
+            values = []
+            for tile in range(2):
+                cells = pl.ds(tile * LANES, LANES)
+                values.append(
+                    (
+                        st[target, one, 0, :, cells] - st[target, two, 1, :, cells],
+                        st[target, one, 1, :, cells] + st[target, two, 0, :, cells],
+                    )
                 )
-                send_buf[target, chunk, 2 * pair + 1] = (
-                    st[target, 2 * pair, 1, :, cells] + st[target, 2 * pair + 1, 0, :, cells]
-                )
-
-        @pl.when(offset > 0)
-        def _():
-            send_piece(target, 0, 0)
-
-        return carry
-
-    lax.fori_loop(0, NAZ, pack, 0)
-    for chunk, pair in ((0, 1), (1, 0), (1, 1)):
-
-        def send_more(offset, carry, chunk=chunk, pair=pair):
-            send_piece(az_target(offset), chunk, pair)
+            for comp in range(2):
+                first, second = values[0][comp], values[1][comp]
+                send_buf[target, 0, pair, comp] = jnp.where(low_lanes, first, second)
+                send_buf[target, 1, pair, comp] = jnp.where(low_lanes, second, first)
+        return carry
+
+    early = 6
+    lax.fori_loop(0, early, pack, 0)
+    pl.semaphore_wait(barrier, NAZ - 1 + NAX - 1)
+
+    def send_modes(offset, carry):
+        pltpu.make_async_remote_copy(
+            src_ref=mode_buf.at[az], dst_ref=mode_buf.at[az], send_sem=m_send, recv_sem=m_recv,
+            device_id=(ax, az_target(offset)), device_id_type=MESH,
+        ).start()
+        return carry
+
+    lax.fori_loop(1, NAZ, send_modes, 0)
+
+    def send_piece(target, chunk, pair, comp):
+        pltpu.make_async_remote_copy(
+            src_ref=send_buf.at[target, chunk, pair, comp],
+            dst_ref=x_buf.at[chunk, pair, comp, pl.ds(az * SLOTS, SLOTS), :],
+            send_sem=f_send, recv_sem=f_recv.at[2 * chunk + pair],
+            device_id=(ax, target), device_id_type=MESH,
+        ).start()
+
+    def send_first(offset, carry):
+        send_piece(az_target(offset), 0, 0, 0)
+        return carry
+
+    lax.fori_loop(1, early, send_first, 0)
+
+    def pack_send(offset, carry):
+        pack(offset, carry)
+        return send_first(offset, carry)
+
+    lax.fori_loop(early, NAZ, pack_send, 0)
+
+    def send_rest(piece, carry):
+        def send_more(offset, carry):
+            send_piece(az_target(offset), lax.div(piece, 4), lax.rem(lax.div(piece, 2), 2), lax.rem(piece, 2))
             return carry
 
-        lax.fori_loop(1, NAZ, send_more, 0)
-
-    def own_copy(chunk):
-        return pltpu.make_async_copy(
-            send_buf.at[az, chunk],
-            x_buf.at[chunk, :, pl.ds(az * SLOTS, SLOTS), :],
-            own_x.at[chunk],
-        )
-
-    own_copy(0).start()
-    own_copy(1).start()
+        return lax.fori_loop(1, NAZ, send_more, carry)
+
+    lax.fori_loop(1, 8, send_rest, 0)
+
+    own_copy = pltpu.make_async_copy(
+        send_buf.at[az], x_buf.at[:, :, :, pl.ds(az * SLOTS, SLOTS), :], own_x
+    )
+    own_copy.start()
 
     courant = courant_ref[...]
-    log_weight = -jnp.log(1.0 + 1.0 / courant)
+    weight = courant / (1.0 + courant)
+    gap = 1.0 - weight
+    series = gap * (
+        1.0 + gap * (1.0 / 2 + gap * (1.0 / 3 + gap * (1.0 / 4 + gap * (1.0 / 5 + gap * (1.0 / 6)))))
+    )
+    log_weight = jnp.where(gap < 0.05, -series, jnp.log(weight))
     row_ids = lax.broadcasted_iota(jnp.int32, (CELLS, CELLS), 0)
     col_ids = lax.broadcasted_iota(jnp.int32, (CELLS, CELLS), 1)
     upper = jnp.where(row_ids <= col_ids, 1.0, 0.0)
@@ -184,7 +202,7 @@
     lc_ref[...] = log_cum
     reach_ref[...] = jnp.exp(log_cum)
     lc_t[...] = jnp.concatenate([log_cum] * 8, axis=0).T
-    om_t[...] = jnp.concatenate([1.0 / (1.0 + courant)] * 8, axis=0).T
+    om_t[...] = jnp.concatenate([gap] * 8, axis=0).T
 
     def build_transfer(radial, scale):
         row = lc_ref[pl.ds(radial, 1), :]
@@ -265,80 +283,9 @@
         buf[pl.ds(pl.multiple_of(HALF + start, SLOTS), SLOTS), lanes] = low
         buf[pl.ds(pl.multiple_of(2 * HALF + start, SLOTS), SLOTS), lanes] = high
 
-    def forward(chunk, carry):
-        own_copy(chunk).wait()
-        arrived = x_buf.at[chunk, :, pl.ds(0, (NAZ - 1) * SLOTS), :]
-        pltpu.make_async_copy(arrived, arrived, f_recv.at[chunk]).wait()
-
-        def fold(block, sums):
-            modes = mode_sub[pl.ds(pl.multiple_of(block * SLOTS, SLOTS), SLOTS), :]
-            alone = is_self(modes)
-            parity = jnp.where((modes.astype(jnp.int32) & 1) == 1, -norm, norm)
-            out = []
-            for comp in range(4):
-                one = x_buf[chunk, comp, pl.ds(pl.multiple_of(block * SLOTS, SLOTS), SLOTS), :]
-                two = x_buf[chunk, comp, pl.ds(pl.multiple_of(HALF + block * SLOTS, SLOTS), SLOTS), :]
-                even = one + (1.0 - alone) * two
-                odd = (one - two) if comp % 2 == 1 else (two - one)
-                put_rhs(rhs_a, block, pl.ds(comp * LANES, LANES), even)
-                put_rhs(rhs_b, block, pl.ds((comp ^ 1) * LANES, LANES), odd)
-                out.append(sums[comp] + fold_rows(alone * two))
-                out.append(sums[4 + comp] + fold_rows(parity * even))
-            return tuple(out[0::2] + out[1::2])
-
-        zero = jnp.zeros((8, LANES), F32)
-        sums = lax.fori_loop(0, HALF // SLOTS, fold, (zero,) * 8)
-        alone_rows = [jnp.sum(sums[c], axis=0, keepdims=True) for c in range(4)]
-        for c in range(4):
-            middle = jnp.sum(sums[4 + c], axis=0, keepdims=True) + alone_rows[c] * norm
-            fmid[chunk, c] = jnp.broadcast_to(middle, (8, LANES))
-        for pair in range(2):
-            lanes = slice(pair * 2 * LANES, (pair + 1) * 2 * LANES)
-            fp[chunk, 2 * pair : 2 * pair + 2] = jnp.stack(
-                jnp.split(
-                    jnp.dot(cos_f[...], rhs_a[:, lanes], preferred_element_type=F32), 2, axis=1
-                )
-            )
-            fm[chunk, 2 * pair : 2 * pair + 2] = jnp.stack(
-                jnp.split(
-                    jnp.dot(sin_f[...], rhs_b[:, lanes], preferred_element_type=F32), 2, axis=1
-                )
-            )
-
-        def combine(block, carry):
-            rows = pl.ds(pl.multiple_of(block * SLOTS, SLOTS), SLOTS)
-            second = second_cos(SLOTS, block * SLOTS)
-            for c in range(4):
-                even = fp[chunk, c, rows, :] + second * alone_rows[c]
-                odd = fm[chunk, c, rows, :]
-                fp[chunk, c, rows, :] = even - odd
-                fm[chunk, c, rows, :] = even + odd
-            return carry
-
-        lax.fori_loop(0, HALF // SLOTS, combine, 0)
-        return carry
-
-    lax.fori_loop(0, 2, forward, 0)
-
     lane64 = lax.broadcasted_iota(jnp.int32, (SLOTS, LANES), 1)
     lane8 = lax.broadcasted_iota(jnp.int32, (8, LANES), 1)
-
-    def edges(block, carry):
-        rows = pl.ds(pl.multiple_of(block * SLOTS, SLOTS), SLOTS)
-        for side, chunk, lane in ((0, 1, LANES - 1), (1, 0, 0)):
-            tile = jnp.zeros((SLOTS, LANES), F32)
-            for c in range(4):
-                tile = jnp.where(lane64 == c, fp[chunk, c, rows, lane : lane + 1], tile)
-                tile = jnp.where(lane64 == 4 + c, fm[chunk, c, rows, lane : lane + 1], tile)
-            halo_send[side, rows, :] = tile
-        return carry
-
-    lax.fori_loop(0, HALF // SLOTS, edges, 0)
-    for side, chunk, lane in ((0, 1, LANES - 1), (1, 0, 0)):
-        tile = jnp.zeros((8, LANES), F32)
-        for c in range(4):
-            tile = jnp.where(lane8 == c, fmid[chunk, c, :, lane : lane + 1], tile)
-        halo_send[side, pl.ds(HALF, 8), :] = tile
+    own_copy.wait()
 
     def halo_copy(side):
         return pltpu.make_async_remote_copy(
@@ -347,8 +294,82 @@
             device_id=(ax_target(1 if side == 0 else NAX - 1), az), device_id_type=MESH,
         )
 
-    halo_copy(0).start()
-    halo_copy(1).start()
+    def send_edges():
+        def edges(block, carry):
+            rows = pl.ds(pl.multiple_of(block * SLOTS, SLOTS), SLOTS)
+            for side, lane in ((0, LANES - 1), (1, 0)):
+                tile = jnp.zeros((SLOTS, LANES), F32)
+                for c in range(4):
+                    tile = jnp.where(lane64 == c, fp[0, c, rows, lane : lane + 1], tile)
+                    tile = jnp.where(lane64 == 4 + c, fm[0, c, rows, lane : lane + 1], tile)
+                halo_send[side, rows, :] = tile
+            return carry
+
+        lax.fori_loop(0, HALF // SLOTS, edges, 0)
+        for side, lane in ((0, LANES - 1), (1, 0)):
+            tile = jnp.zeros((8, LANES), F32)
+            for c in range(4):
+                tile = jnp.where(lane8 == c, fmid[0, c, :, lane : lane + 1], tile)
+            halo_send[side, pl.ds(HALF, 8), :] = tile
+        halo_copy(0).start()
+        halo_copy(1).start()
+
+    def forward(unit, carry):
+        chunk = lax.div(unit, 2)
+        pair = lax.rem(unit, 2)
+        arrived = x_buf.at[chunk, pair, :, pl.ds(0, (NAZ - 1) * SLOTS), :]
+        pltpu.make_async_copy(arrived, arrived, f_recv.at[unit]).wait()
+
+        def fold(block, sums):
+            modes = mode_sub[pl.ds(pl.multiple_of(block * SLOTS, SLOTS), SLOTS), :]
+            alone = is_self(modes)
+            parity = jnp.where((modes.astype(jnp.int32) & 1) == 1, -norm, norm)
+            out = []
+            for comp in range(2):
+                one = x_buf[chunk, pair, comp, pl.ds(pl.multiple_of(block * SLOTS, SLOTS), SLOTS), :]
+                two = x_buf[
+                    chunk, pair, comp, pl.ds(pl.multiple_of(HALF + block * SLOTS, SLOTS), SLOTS), :
+                ]
+                even = one + (1.0 - alone) * two
+                odd = (one - two) if comp % 2 == 1 else (two - one)
+                put_rhs(rhs_a, block, pl.ds(comp * LANES, LANES), even)
+                put_rhs(rhs_b, block, pl.ds((comp ^ 1) * LANES, LANES), odd)
+                out.append(sums[comp] + fold_rows(alone * two))
+                out.append(sums[2 + comp] + fold_rows(parity * even))
+            return tuple(out[0::2] + out[1::2])
+
+        zero = jnp.zeros((8, LANES), F32)
+        sums = lax.fori_loop(0, HALF // SLOTS, fold, (zero,) * 4)
+        alone_rows = [jnp.sum(sums[c], axis=0, keepdims=True) for c in range(2)]
+        for c in range(2):
+            middle = jnp.sum(sums[2 + c], axis=0, keepdims=True) + alone_rows[c] * norm
+            fmid[chunk, 2 * pair + c] = jnp.broadcast_to(middle, (8, LANES))
+        cos_sum = jnp.dot(cos_f[...], rhs_a[:, 0:CELLS], preferred_element_type=F32)
+        sin_sum = jnp.dot(sin_f[...], rhs_b[:, 0:CELLS], preferred_element_type=F32)
+        for c in range(2):
+            lanes = slice(c * LANES, (c + 1) * LANES)
+            fp[chunk, 2 * pair + c] = cos_sum[:, lanes]
+            fm[chunk, 2 * pair + c] = sin_sum[:, lanes]
+
+        def combine(block, carry):
+            rows = pl.ds(pl.multiple_of(block * SLOTS, SLOTS), SLOTS)
+            second = second_cos(SLOTS, block * SLOTS)
+            for c in range(2):
+                even = fp[chunk, 2 * pair + c, rows, :] + second * alone_rows[c]
+                odd = fm[chunk, 2 * pair + c, rows, :]
+                fp[chunk, 2 * pair + c, rows, :] = even - odd
+                fm[chunk, 2 * pair + c, rows, :] = even + odd
+            return carry
+
+        lax.fori_loop(0, HALF // SLOTS, combine, 0)
+
+        @pl.when(unit == 1)
+        def _():
+            send_edges()
+
+        return carry
+
+    lax.fori_loop(0, 4, forward, 0)
     halo_copy(0).wait()
     halo_copy(1).wait()
     left_on = jnp.where(ax > 0, 1.0, 0.0)
@@ -357,9 +378,14 @@
     here_square = here * here
 
     def flux_pair(get, rows, c, left_lane0, left_lanec, cell):
-        first = jnp.concatenate([get(0, 0), get(1, 0)], axis=1)
-        this = jnp.concatenate([get(0, c), get(1, c)], axis=1)
-        third = jnp.concatenate([get(0, 2), get(1, 2)], axis=1)
+        def cells(field):
+            outer, inner = get(0, field), get(1, field)
+            low_lanes = (lane64 if rows is not None else lane8) < LANES // 2
+            return jnp.concatenate(
+                [jnp.where(low_lanes, outer, inner), jnp.where(low_lanes, inner, outer)], axis=1
+            )
+
+        first, this, third = cells(0), cells(c), cells(2)
         axial = first * this
         after = pltpu.roll(axial, CELLS - 1, axis=1)
         before = pltpu.roll(axial, 1, axis=1)
@@ -370,6 +396,13 @@
 
     def pick_lane(tile, lanes, index):
         return jnp.sum(jnp.where(lanes == index, tile, 0.0), axis=1, keepdims=True)
+
+    def own_back(c):
+        return pltpu.make_async_copy(
+            e_send.at[c, :, :, pl.ds(lax.rem(az, 8) * SLOTS, SLOTS), :],
+            e_recv.at[c, :, az],
+            own_e.at[c],
+        )
 
     def explicit(c, carry):
         def fluxes(block, sums):
@@ -439,26 +472,30 @@
 
         lax.fori_loop(0, HALF // SLOTS, finish, 0)
         for part in range(2):
-            e_send[c, part] = jnp.dot(
+            swept = jnp.dot(
                 lhs_cat[part * HALF : (part + 1) * HALF, :], tcat[...], preferred_element_type=F32
             )
-        pltpu.make_async_copy(
-            e_send.at[c, :, pl.ds(lax.rem(az, 8) * SLOTS, SLOTS), :], e_recv.at[c, az], own_e.at[c]
-        ).start()
-
-        for part in range(2):
-
-            def send_back(offset, carry, part=part):
+            for tile in range(2):
+                e_send[c, tile, part] = swept[:, tile * LANES : (tile + 1) * LANES]
+        own_back(c).start()
+
+        def send_piece_back(piece, carry):
+            tile = 1 - lax.div(piece, 2)
+            part = lax.rem(piece, 2)
+
+            def send_back(offset, carry):
                 target = az_target(offset)
                 pltpu.make_async_remote_copy(
-                    src_ref=e_send.at[c, part, pl.ds(lax.rem(target, 8) * SLOTS, SLOTS), :],
-                    dst_ref=e_recv.at[c, az, part],
-                    send_sem=e_send_sem, recv_sem=e_recv_sem.at[c],
+                    src_ref=e_send.at[c, tile, part, pl.ds(lax.rem(target, 8) * SLOTS, SLOTS), :],
+                    dst_ref=e_recv.at[c, tile, az, part],
+                    send_sem=e_send_sem, recv_sem=e_recv_sem.at[2 * c + tile],
                     device_id=(ax, target), device_id_type=MESH,
                 ).start()
                 return carry
 
-            lax.fori_loop(1, NAZ, send_back, 0)
+            return lax.fori_loop(1, NAZ, send_back, carry)
+
+        lax.fori_loop(0, 4, send_piece_back, 0)
         return carry
 
     lax.fori_loop(0, FIELDS, explicit, 0)
@@ -486,34 +523,6 @@
     own_alone = is_self(own_sub[...])
     swap = own_alone * (1.0 - low_half)
     flip = (1.0 - own_alone) * (2.0 * low_half - 1.0)
-    swap = jnp.concatenate([swap, swap], axis=1)
-    flip = jnp.concatenate([flip, flip], axis=1)
-
-    def arrive(c, last):
-        pltpu.make_async_copy(
-            e_send.at[c, :, pl.ds(lax.rem(az, 8) * SLOTS, SLOTS), :], e_recv.at[c, az], own_e.at[c]
-        ).wait()
-        arrived = e_recv.at[c, pl.ds(0, NAZ - 1)]
-        pltpu.make_async_copy(arrived, arrived, e_recv_sem.at[c]).wait()
-
-        def add(radial, last):
-            real = e_recv[c, radial, 0]
-            imag = e_recv[c, radial, 1]
-            new_real = st[radial, c, 0] + real + swap * (imag - real)
-            new_imag = st[radial, c, 1] + flip * imag
-            st[radial, c, 0] = new_real
-            st[radial, c, 1] = new_imag
-            where = c * 2 * NR + radial
-            last = jnp.where(lane64 == where, new_real[:, CELLS - 1 : CELLS], last)
-            last = jnp.where(lane64 == where + NR, new_imag[:, CELLS - 1 : CELLS], last)
-            pltpu.make_async_copy(st.at[radial, c], acc_ref.at[c, :, radial], out_sem.at[c]).start()
-            return last
-
-        return lax.fori_loop(0, NR, add, last)
-
-    last = lax.fori_loop(0, FIELDS, arrive, jnp.zeros((SLOTS, LANES), F32))
-
-    rel_buf[ax, pl.ds(0, SLOTS), :] = last
     decay_row = jnp.exp(lc_t[pl.ds(CELLS - 8, 8), :])[7:8, :]
     rel_buf[ax, pl.ds(SLOTS, 8), :] = jnp.broadcast_to(decay_row, (8, LANES))
 
@@ -524,7 +533,48 @@
         ).start()
         return carry
 
-    lax.fori_loop(1, NAX, send_last, 0)
+    def arrive(c, last):
+        own_back(c).wait()
+
+        def add(tile, radial):
+            lanes = pl.ds(tile * LANES, LANES)
+            real = e_recv[c, tile, radial, 0]
+            imag = e_recv[c, tile, radial, 1]
+            new_real = st[radial, c, 0, :, lanes] + real + swap * (imag - real)
+            new_imag = st[radial, c, 1, :, lanes] + flip * imag
+            st[radial, c, 0, :, lanes] = new_real
+            st[radial, c, 1, :, lanes] = new_imag
+            return new_real, new_imag
+
+        def landed(tile):
+            ref = e_recv.at[c, tile, pl.ds(0, NAZ - 1)]
+            pltpu.make_async_copy(ref, ref, e_recv_sem.at[2 * c + tile]).wait()
+
+        def add_last(radial, last):
+            new_real, new_imag = add(1, radial)
+            where = c * 2 * NR + radial
+            last = jnp.where(lane64 == where, new_real[:, LANES - 1 : LANES], last)
+            return jnp.where(lane64 == where + NR, new_imag[:, LANES - 1 : LANES], last)
+
+        def add_first(radial, carry):
+            add(0, radial)
+            pltpu.make_async_copy(st.at[radial, c], acc_ref.at[c, :, radial], out_sem.at[c]).start()
+            return carry
+
+        landed(1)
+        last = lax.fori_loop(0, NR, add_last, last)
+
+        @pl.when(c == FIELDS - 1)
+        def _():
+            rel_buf[ax, pl.ds(0, SLOTS), :] = last
+            lax.fori_loop(1, NAX, send_last, 0)
+
+        landed(0)
+        lax.fori_loop(0, NR, add_first, 0)
+        return last
+
+    lax.fori_loop(0, FIELDS, arrive, jnp.zeros((SLOTS, LANES), F32))
+
     others = rel_buf.at[pl.ds(0, NAX - 1)]
     pltpu.make_async_copy(others, others, rel_recv).wait()
 
@@ -533,7 +583,10 @@
         decay = rel_buf[block, pl.ds(SLOTS, 8), :][0:1, :]
         return jnp.where(block < ax, decay * incoming + upstream, incoming)
 
-    incoming_ref[...] = lax.fori_loop(0, NAX - 1, relay, inflow_ref[...])
+    inflow = inflow_ref[...]
+    inflow = jnp.concatenate([inflow, inflow], axis=1).T[:SLOTS, :]
+    incoming = lax.fori_loop(0, NAX - 1, relay, inflow)
+    incoming_ref[...] = jnp.concatenate([incoming, incoming], axis=0).T[:, :SLOTS]
 
     pltpu.make_async_copy(others, others, rel_send).wait()
     pltpu.make_async_copy(
@@ -541,7 +594,7 @@
     ).wait()
     sent = send_buf.at[pl.ds(0, NAZ - 1)]
     pltpu.make_async_copy(sent, sent, f_send).wait()
-    sent_back = e_recv.at[:, pl.ds(0, NAZ - 1)]
+    sent_back = e_recv.at[:, :, pl.ds(0, NAZ - 1)]
     pltpu.make_async_copy(sent_back, sent_back, e_send_sem).wait()
 
     def written(c, carry):
@@ -552,15 +605,15 @@
 
 
 def shards(state, inflow, courant, mode_number, partner_table):
-    modes = jnp.broadcast_to(jnp.concatenate([mode_number, mode_number])[None, :], (8, LANES))
-    inflow_tile = inflow.reshape(FIELDS * 2 * NR, SLOTS).T
+    modes = mode_number.reshape(1, SLOTS)
+    inflow_rows = inflow.reshape(FIELDS * 2 * NR, SLOTS)
     dma = pltpu.SemaphoreType.DMA
     vmem = pltpu.VMEM
     acc, incoming, reach = pl.pallas_call(
         kernel,
         out_shape=(
             jax.ShapeDtypeStruct((FIELDS, 2, NR, SLOTS, CELLS), F32),
-            jax.ShapeDtypeStruct((SLOTS, LANES), F32),
+            jax.ShapeDtypeStruct((FIELDS * 2 * NR, SLOTS), F32),
             jax.ShapeDtypeStruct((NR, CELLS), F32),
         ),
         in_specs=[
@@ -576,8 +629,8 @@
         ),
         scratch_shapes=[
             vmem((NR, FIELDS, 2, SLOTS, CELLS), F32),
-            vmem((NAZ, 2, 4, SLOTS, LANES), F32),
-            vmem((2, 4, M, LANES), F32),
+            vmem((NAZ, 2, 2, 2, SLOTS, LANES), F32),
+            vmem((2, 2, 2, M, LANES), F32),
             vmem((NAZ, 8, LANES), jnp.int32),
             vmem((HALF, LANES), F32),
             vmem((SLOTS, LANES), F32),
@@ -591,27 +644,26 @@
             vmem((2, FIELDS, HALF, LANES), F32),
             vmem((2, FIELDS, HALF, LANES), F32),
             vmem((2, FIELDS, 8, LANES), F32),
-            vmem((8, LANES), F32),
             vmem((2, HALF + 8, LANES), F32),
             vmem((2, HALF + 8, LANES), F32),
             vmem((NR, CELLS), F32),
             vmem((CELLS, LANES), F32),
             vmem((CELLS, LANES), F32),
             vmem((4, HALF, CELLS), F32),
-            vmem((FIELDS, 2, HALF, CELLS), F32),
-            vmem((FIELDS, NAZ, 2, SLOTS, CELLS), F32),
+            vmem((FIELDS, 2, 2, HALF, LANES), F32),
+            vmem((FIELDS, 2, NAZ, 2, SLOTS, LANES), F32),
             vmem((M, 3 * CELLS), BF16),
             vmem((NAX, SLOTS + 8, LANES), F32),
             dma((NAZ,)),
             dma,
-            dma((2,)),
+            dma((4,)),
+            dma,
             dma,
             dma,
             dma((2,)),
             dma((2,)),
-            dma((2,)),
             dma,
-            dma((FIELDS,)),
+            dma((2 * FIELDS,)),
             dma((FIELDS,)),
             dma((FIELDS,)),
             dma,
@@ -620,8 +672,8 @@
         compiler_params=pltpu.CompilerParams(
             collective_id=0, has_side_effects=True, vmem_limit_bytes=58 * 2**20
         ),
-    )(state, courant, modes, inflow_tile)
-    incoming_full = incoming.T.reshape(FIELDS, 2, NR, SLOTS)
+    )(state, courant, modes, inflow_rows)
+    incoming_full = incoming.reshape(FIELDS, 2, NR, SLOTS)
     return acc + reach[None, None, :, None, :] * incoming_full[..., None]
 
 

time: 196 us -> 165 us (0.84); the launches traced: 193 us -> 165 us
  Pallas kernels: 183 us -> 159 us
  local copies, waits for them, and re-layouts: 2.97 us -> 0 us
    pallas_call x1, Pallas kernels: 183 us -> 159 us  [shards(): pl.pallas_call(kernel, out_shape=(jax.ShapeDtypeStruct((FIELDS, 2, NR, SL...]
where the time goes in v2:
time: 165 us
  Pallas kernels  159 us (96%)
  other arithmetic  6.21 us (4%)
    pallas_call x1, Pallas kernels, shards(): pl.pallas_call(kernel, out_shape=(jax.ShapeDtypeStruct((FIELDS, 2, NR, SL...  159 us
    add x1, other arithmetic, shards(): return acc + reach[None, None, :, None, :] * incoming_full[..., None]  6.21 us

profile of v2, /device:TPU:1, one launch (start us, length us, event | category | flops | bytes accessed | tf_op | source)
XLA Modules:
  0.0 164.8 jit_solution(2608272735307534404)
XLA Ops:
  0.0 158.6 %shard_map.46 = (f32[4,2,16,64,256]{4,3,2,1,0:T(8,128)}, f32[128,64]{1,0:T(8,128)}, f32[16,256]{1,0:T(8,128)}) custom-call(f32[4,2,16,64,256]{4,3,2,1,0:T(8,128)} %state_ref.1, f32[16,256]{1,0:T(8,128)} %courant_ref.1, s32[1,64]{1,0:T(1,128)} %bitcast.5, f32[128,64]{1,0:T(8,128)} %bitcast.3), custom_call_target="tpu_custom_call" | custom-call | tf_op jit(solution)/shard_map/pallas_call | solution.py:612
  158.6 6.2 %multiply_add_fusion = f32[4,2,16,64,256]{4,3,2,1,0:T(8,128)} fusion(f32[4,2,16,64,256]{4,3,2,1,0:T(8,128)} %get-tuple-element.8, f32[4,2,16,64]{3,2,1,0:T(8,128)} %bitcast.4, f32[16,256]{1,0:T(8,128)} %get-tuple-element.9), kind=kLoop, calls=%fused_computation | loop fusion | flops 4194304 | bytes 16826368 | tf_op jit(solution)/shard_map/add | solution.py:677

commit v3 on v2

--- a/solution.py
+++ b/solution.py
@@ -72,11 +72,11 @@
 def kernel(
     state_ref, courant_ref, mode_ref, inflow_ref,
     acc_ref, incoming_ref, reach_ref,
-    st, send_buf, x_buf, mode_buf, mode_sub, own_sub,
+    st, send_buf, x_buf, alone_send, alone_recv, alone_sum, mode_buf, mode_sub, own_sub,
     cos_f, sin_f, cos_r, sin_r, rhs_a, rhs_b, tcat,
     fp, fm, fmid, halo_send, halo_recv,
     lc_ref, lc_t, om_t, e_raw, e_send, e_recv, lhs_cat, rel_buf,
-    st_sem, f_send, f_recv, m_send, m_recv, own_x, h_send, h_recv,
+    st_sem, f_send, f_recv, a_send, a_recv, m_send, m_recv, own_x, h_send, h_recv,
     e_send_sem, e_recv_sem, own_e, out_sem, rel_send, rel_recv,
 ):
     ax = lax.axis_index("ax")
@@ -92,7 +92,9 @@
         return lax.rem(ax + offset, NAX)
 
     def start_state(offset, carry):
-        target = az_target(offset)
+        turn = lax.div(offset, 4)
+        step = lax.rem(1 + 2 * turn + lax.div(turn, 2) * 3, 4)
+        target = lax.rem(z + step, 4) * 4 + lax.rem(y + lax.rem(offset, 4), 4)
         pltpu.make_async_copy(
             state_ref.at[:, :, target], st.at[target], st_sem.at[target]
         ).start()
@@ -116,31 +118,39 @@
     modes_here = mode_ref[...]
     mode_buf[az] = jnp.broadcast_to(jnp.concatenate([modes_here, modes_here], axis=1), (8, LANES))
 
-    def pack(offset, carry):
-        target = az_target(offset)
+    own_sub[...] = jnp.concatenate([mode_buf[az].astype(F32)] * 16, axis=0).T[:SLOTS, :]
+
+    group = lax.rem(z, 2) * 4 + y
+    sign = jnp.where(z < 2, 1.0, -1.0)
+    low_lanes = lax.broadcasted_iota(jnp.int32, (SLOTS, LANES), 1) < LANES // 2
+
+    def column(step, dy):
+        return lax.rem(z + step, 4) * 4 + lax.rem(y + dy, 4)
+
+    def state_here(target):
         pltpu.make_async_copy(
             state_ref.at[:, :, target], st.at[target], st_sem.at[target]
         ).wait()
-        low_lanes = lax.broadcasted_iota(jnp.int32, (SLOTS, LANES), 1) < LANES // 2
-        for pair in range(2):
-            one, two = 2 * pair, 2 * pair + 1
-            values = []
-            for tile in range(2):
-                cells = pl.ds(tile * LANES, LANES)
-                values.append(
-                    (
-                        st[target, one, 0, :, cells] - st[target, two, 1, :, cells],
-                        st[target, one, 1, :, cells] + st[target, two, 0, :, cells],
-                    )
-                )
-            for comp in range(2):
-                first, second = values[0][comp], values[1][comp]
-                send_buf[target, 0, pair, comp] = jnp.where(low_lanes, first, second)
-                send_buf[target, 1, pair, comp] = jnp.where(low_lanes, second, first)
-        return carry
-
-    early = 6
-    lax.fori_loop(0, early, pack, 0)
+
+    def pack(step, parts):
+        def body(dy, carry):
+            target = column(step, dy)
+            state_here(target)
+            for field in range(FIELDS):
+                for part in parts:
+                    first = st[target, field, part, :, 0:LANES]
+                    second = st[target, field, part, :, LANES:CELLS]
+                    if part == 1:
+                        first, second = first * sign, second * sign
+                    pair, place = field % 2, field // 2
+                    send_buf[target, 0, pair, place, part] = jnp.where(low_lanes, first, second)
+                    send_buf[target, 1, pair, place, part] = jnp.where(low_lanes, second, first)
+            return carry
+
+        lax.fori_loop(0, 4, body, 0)
+
+    pack(1, (0,))
+    pack(3, (1,))
     pl.semaphore_wait(barrier, NAZ - 1 + NAX - 1)
 
     def send_modes(offset, carry):
@@ -152,37 +162,73 @@
 
     lax.fori_loop(1, NAZ, send_modes, 0)
 
-    def send_piece(target, chunk, pair, comp):
+    def send_piece(chunk, pair, place, index):
+        same = lax.div(index, 8)
+        part = (1 - same) * lax.div(index, 4) + same * lax.rem(index, 2)
+        step = (1 - same) * (1 + 2 * lax.div(index, 4))
+        dy = (1 - same) * lax.rem(index, 4) + same * (lax.div(index, 2) - 3)
+        target = column(step, dy)
         pltpu.make_async_remote_copy(
-            src_ref=send_buf.at[target, chunk, pair, comp],
-            dst_ref=x_buf.at[chunk, pair, comp, pl.ds(az * SLOTS, SLOTS), :],
+            src_ref=send_buf.at[target, chunk, pair, place, part],
+            dst_ref=x_buf.at[chunk, pair, place, part, pl.ds(group * SLOTS, SLOTS), :],
             send_sem=f_send, recv_sem=f_recv.at[2 * chunk + pair],
             device_id=(ax, target), device_id_type=MESH,
         ).start()
 
-    def send_first(offset, carry):
-        send_piece(az_target(offset), 0, 0, 0)
-        return carry
-
-    lax.fori_loop(1, early, send_first, 0)
-
-    def pack_send(offset, carry):
-        pack(offset, carry)
-        return send_first(offset, carry)
-
-    lax.fori_loop(early, NAZ, pack_send, 0)
+    def send_first(index, carry):
+        send_piece(0, 0, 0, index)
+        return carry
+
+    lax.fori_loop(0, 8, send_first, 0)
+    pack(0, (0, 1))
+    lax.fori_loop(8, 14, send_first, 0)
 
     def send_rest(piece, carry):
-        def send_more(offset, carry):
-            send_piece(az_target(offset), lax.div(piece, 4), lax.rem(lax.div(piece, 2), 2), lax.rem(piece, 2))
+        def send_more(count, carry):
+            send_piece(
+                lax.div(piece, 4), lax.rem(lax.div(piece, 2), 2), lax.rem(piece, 2),
+                lax.rem(count * 5, 14),
+            )
             return carry
 
-        return lax.fori_loop(1, NAZ, send_more, carry)
-
-    lax.fori_loop(1, 8, send_rest, 0)
+        return lax.fori_loop(0, 14, send_more, carry)
+
+    lax.fori_loop(1, 2, send_rest, 0)
+
+    own_alone = is_self(own_sub[...])
+
+    def alone_there(dy, carry):
+        state_here(column(2, dy))
+        return carry
+
+    lax.fori_loop(0, 4, alone_there, 0)
+
+    def alone_row(radial, carry):
+        rows = [[], []]
+        for field in range(FIELDS):
+            first = jnp.sum(own_alone * st[radial, field, 0, :, 0:LANES], axis=0, keepdims=True)
+            second = jnp.sum(own_alone * st[radial, field, 0, :, LANES:CELLS], axis=0, keepdims=True)
+            rows[0].append(jnp.where(low_lanes[0:1], first, second))
+            rows[1].append(jnp.where(low_lanes[0:1], second, first))
+        alone_send[radial] = jnp.concatenate(rows[0] + rows[1], axis=0)
+        return carry
+
+    lax.fori_loop(0, NR, alone_row, 0)
+    alone_recv[az] = alone_send[az]
+
+    def send_alone(offset, carry):
+        target = az_target(offset)
+        pltpu.make_async_remote_copy(
+            src_ref=alone_send.at[target], dst_ref=alone_recv.at[az], send_sem=a_send,
+            recv_sem=a_recv, device_id=(ax, target), device_id_type=MESH,
+        ).start()
+        return carry
+
+    lax.fori_loop(1, NAZ, send_alone, 0)
+    lax.fori_loop(2, 8, send_rest, 0)
 
     own_copy = pltpu.make_async_copy(
-        send_buf.at[az], x_buf.at[:, :, :, pl.ds(az * SLOTS, SLOTS), :], own_x
+        send_buf.at[az], x_buf.at[:, :, :, :, pl.ds(group * SLOTS, SLOTS), :], own_x
     )
     own_copy.start()
 
@@ -236,7 +282,6 @@
     for q in range(4):
         wide = jnp.concatenate([mode_lane[q].astype(F32)] * 16, axis=0)
         mode_sub[pl.ds(q * LANES, LANES), :] = wide.T
-    own_sub[...] = jnp.concatenate([mode_buf[az].astype(F32)] * 16, axis=0).T[:SLOTS, :]
     mode_row = jnp.concatenate(mode_lane, axis=1)[0:1, :]
 
     def tables(block, carry):
@@ -286,6 +331,15 @@
     lane64 = lax.broadcasted_iota(jnp.int32, (SLOTS, LANES), 1)
     lane8 = lax.broadcasted_iota(jnp.int32, (8, LANES), 1)
     own_copy.wait()
+    pltpu.make_async_copy(alone_send.at[pl.ds(0, NAZ - 1)], alone_recv.at[pl.ds(0, NAZ - 1)], a_recv).wait()
+
+    def add_alone(source, total):
+        return total + alone_recv[source]
+
+    for half in range(2):
+        alone_sum[half] = lax.fori_loop(
+            half * (NAZ // 2), (half + 1) * (NAZ // 2), add_alone, jnp.zeros((8, LANES), F32)
+        )
 
     def halo_copy(side):
         return pltpu.make_async_remote_copy(
@@ -317,48 +371,49 @@
     def forward(unit, carry):
         chunk = lax.div(unit, 2)
         pair = lax.rem(unit, 2)
-        arrived = x_buf.at[chunk, pair, :, pl.ds(0, (NAZ - 1) * SLOTS), :]
+        arrived = x_buf.at[chunk, pair, :, :, pl.ds(0, 7 * SLOTS), :]
         pltpu.make_async_copy(arrived, arrived, f_recv.at[unit]).wait()
 
         def fold(block, sums):
-            modes = mode_sub[pl.ds(pl.multiple_of(block * SLOTS, SLOTS), SLOTS), :]
-            alone = is_self(modes)
+            rows = pl.ds(pl.multiple_of(block * SLOTS, SLOTS), SLOTS)
+            modes = mode_sub[rows, :]
+            double = 2.0 - 2.0 * is_self(modes)
             parity = jnp.where((modes.astype(jnp.int32) & 1) == 1, -norm, norm)
             out = []
-            for comp in range(2):
-                one = x_buf[chunk, pair, comp, pl.ds(pl.multiple_of(block * SLOTS, SLOTS), SLOTS), :]
-                two = x_buf[
-                    chunk, pair, comp, pl.ds(pl.multiple_of(HALF + block * SLOTS, SLOTS), SLOTS), :
-                ]
-                even = one + (1.0 - alone) * two
-                odd = (one - two) if comp % 2 == 1 else (two - one)
-                put_rhs(rhs_a, block, pl.ds(comp * LANES, LANES), even)
-                put_rhs(rhs_b, block, pl.ds((comp ^ 1) * LANES, LANES), odd)
-                out.append(sums[comp] + fold_rows(alone * two))
-                out.append(sums[2 + comp] + fold_rows(parity * even))
-            return tuple(out[0::2] + out[1::2])
+            for place in range(2):
+                even = double * x_buf[chunk, pair, place, 0, rows, :]
+                odd = 2.0 * x_buf[chunk, pair, place, 1, rows, :]
+                put_rhs(rhs_a, block, pl.ds(place * LANES, LANES), even)
+                put_rhs(rhs_b, block, pl.ds(place * LANES, LANES), odd)
+                out.append(sums[place] + fold_rows(parity * even))
+            return tuple(out)
 
         zero = jnp.zeros((8, LANES), F32)
-        sums = lax.fori_loop(0, HALF // SLOTS, fold, (zero,) * 4)
-        alone_rows = [jnp.sum(sums[c], axis=0, keepdims=True) for c in range(2)]
-        for c in range(2):
-            middle = jnp.sum(sums[2 + c], axis=0, keepdims=True) + alone_rows[c] * norm
-            fmid[chunk, 2 * pair + c] = jnp.broadcast_to(middle, (8, LANES))
+        sums = lax.fori_loop(0, HALF // SLOTS, fold, (zero,) * 2)
+        first_rows = [alone_sum[0, pl.ds(4 * chunk + pair + 2 * place, 1), :] for place in range(2)]
+        second_rows = [alone_sum[1, pl.ds(4 * chunk + pair + 2 * place, 1), :] for place in range(2)]
+        for place in range(2):
+            middle = jnp.sum(sums[place], axis=0, keepdims=True)
+            middle = middle + (first_rows[place] + second_rows[place]) * norm
+            fmid[chunk, pair + 2 * place] = jnp.broadcast_to(middle, (8, LANES))
         cos_sum = jnp.dot(cos_f[...], rhs_a[:, 0:CELLS], preferred_element_type=F32)
         sin_sum = jnp.dot(sin_f[...], rhs_b[:, 0:CELLS], preferred_element_type=F32)
         for c in range(2):
             lanes = slice(c * LANES, (c + 1) * LANES)
-            fp[chunk, 2 * pair + c] = cos_sum[:, lanes]
-            fm[chunk, 2 * pair + c] = sin_sum[:, lanes]
+            fp[chunk, pair + 2 * c] = cos_sum[:, lanes]
+            fm[chunk, pair + 2 * c] = sin_sum[:, lanes]
 
         def combine(block, carry):
             rows = pl.ds(pl.multiple_of(block * SLOTS, SLOTS), SLOTS)
-            second = second_cos(SLOTS, block * SLOTS)
+            point = block * SLOTS + lax.broadcasted_iota(jnp.int32, (SLOTS, LANES), 0)
+            first = jnp.where((~second_is_half) & ((point & 1) == 1), -norm, norm)
+            second = jnp.where(second_is_half & ((point & 1) == 1), -norm, norm)
             for c in range(2):
-                even = fp[chunk, 2 * pair + c, rows, :] + second * alone_rows[c]
-                odd = fm[chunk, 2 * pair + c, rows, :]
-                fp[chunk, 2 * pair + c, rows, :] = even - odd
-                fm[chunk, 2 * pair + c, rows, :] = even + odd
+                even = fp[chunk, pair + 2 * c, rows, :] + first * first_rows[c]
+                even = even + second * second_rows[c]
+                odd = fm[chunk, pair + 2 * c, rows, :]
+                fp[chunk, pair + 2 * c, rows, :] = even - odd
+                fm[chunk, pair + 2 * c, rows, :] = even + odd
             return carry
 
         lax.fori_loop(0, HALF // SLOTS, combine, 0)
@@ -369,7 +424,7 @@
 
         return carry
 
-    lax.fori_loop(0, 4, forward, 0)
+    lax.fori_loop(0, 3, forward, 0)
     halo_copy(0).wait()
     halo_copy(1).wait()
     left_on = jnp.where(ax > 0, 1.0, 0.0)
@@ -404,7 +459,13 @@
             own_e.at[c],
         )
 
-    def explicit(c, carry):
+    def explicit(turn, carry):
+        c = lax.rem(turn, 2) * 2 + lax.div(turn, 2)
+
+        @pl.when(turn == 2)
+        def _():
+            forward(3, 0)
+
         def fluxes(block, sums):
             rows = pl.ds(pl.multiple_of(block * SLOTS, SLOTS), SLOTS)
             cell = lax.broadcasted_iota(jnp.int32, (SLOTS, CELLS), 1)
@@ -520,7 +581,6 @@
     lax.fori_loop(0, NR, state_sweep, 0)
 
     low_half = jnp.where(z < 2, 1.0, 0.0)
-    own_alone = is_self(own_sub[...])
     swap = own_alone * (1.0 - low_half)
     flip = (1.0 - own_alone) * (2.0 * low_half - 1.0)
     decay_row = jnp.exp(lc_t[pl.ds(CELLS - 8, 8), :])[7:8, :]
@@ -533,7 +593,8 @@
         ).start()
         return carry
 
-    def arrive(c, last):
+    def arrive(turn, last):
+        c = lax.rem(turn, 2) * 2 + lax.div(turn, 2)
         own_back(c).wait()
 
         def add(tile, radial):
@@ -592,7 +653,9 @@
     pltpu.make_async_copy(
         mode_buf.at[pl.ds(0, NAZ - 1)], mode_buf.at[pl.ds(0, NAZ - 1)], m_send
     ).wait()
-    sent = send_buf.at[pl.ds(0, NAZ - 1)]
+    alone_sent = alone_recv.at[pl.ds(0, NAZ - 1)]
+    pltpu.make_async_copy(alone_sent, alone_sent, a_send).wait()
+    sent = x_buf.at[:, :, :, :, pl.ds(0, 7 * SLOTS), :]
     pltpu.make_async_copy(sent, sent, f_send).wait()
     sent_back = e_recv.at[:, :, pl.ds(0, NAZ - 1)]
     pltpu.make_async_copy(sent_back, sent_back, e_send_sem).wait()
@@ -629,8 +692,11 @@
         ),
         scratch_shapes=[
             vmem((NR, FIELDS, 2, SLOTS, CELLS), F32),
-            vmem((NAZ, 2, 2, 2, SLOTS, LANES), F32),
-            vmem((2, 2, 2, M, LANES), F32),
+            vmem((NAZ, 2, 2, 2, 2, SLOTS, LANES), F32),
+            vmem((2, 2, 2, 2, HALF, LANES), F32),
+            vmem((NAZ, 8, LANES), F32),
+            vmem((NAZ, 8, LANES), F32),
+            vmem((2, 8, LANES), F32),
             vmem((NAZ, 8, LANES), jnp.int32),
             vmem((HALF, LANES), F32),
             vmem((SLOTS, LANES), F32),
@@ -660,6 +726,8 @@
             dma,
             dma,
             dma,
+            dma,
+            dma,
             dma((2,)),
             dma((2,)),
             dma,

time: 165 us -> 157 us (0.952)
  Pallas kernels: 159 us -> 151 us
    pallas_call x1, Pallas kernels: 159 us -> 151 us  [shards(): pl.pallas_call(kernel, out_shape=(jax.ShapeDtypeStruct((FIELDS, 2, NR, SL...]
where the time goes in v3:
time: 157 us
  Pallas kernels  151 us (96%)
  other arithmetic  6.21 us (4%)
    pallas_call x1, Pallas kernels, shards(): pl.pallas_call(kernel, out_shape=(jax.ShapeDtypeStruct((FIELDS, 2, NR, SL...  151 us
    add x1, other arithmetic, shards(): return acc + reach[None, None, :, None, :] * incoming_full[..., None]  6.21 us

profile of v3, /device:TPU:1, one launch (start us, length us, event | category | flops | bytes accessed | tf_op | source)
XLA Modules:
  0.0 157.0 jit_solution(5806707839392297827)
XLA Ops:
  0.0 150.8 %shard_map.46 = (f32[4,2,16,64,256]{4,3,2,1,0:T(8,128)}, f32[128,64]{1,0:T(8,128)}, f32[16,256]{1,0:T(8,128)}) custom-call(f32[4,2,16,64,256]{4,3,2,1,0:T(8,128)} %state_ref.1, f32[16,256]{1,0:T(8,128)} %courant_ref.1, s32[1,64]{1,0:T(1,128)} %bitcast.5, f32[128,64]{1,0:T(8,128)} %bitcast.3), custom_call_target="tpu_custom_call" | custom-call | tf_op jit(solution)/shard_map/pallas_call | solution.py:675
  150.8 6.2 %multiply_add_fusion = f32[4,2,16,64,256]{4,3,2,1,0:T(8,128)} fusion(f32[4,2,16,64,256]{4,3,2,1,0:T(8,128)} %get-tuple-element.8, f32[4,2,16,64]{3,2,1,0:T(8,128)} %bitcast.4, f32[16,256]{1,0:T(8,128)} %get-tuple-element.9), kind=kLoop, calls=%fused_computation | loop fusion | flops 4194304 | bytes 16826368 | tf_op jit(solution)/shard_map/add | solution.py:745

commit v4 on v3

--- a/solution.py
+++ b/solution.py
@@ -171,7 +171,7 @@
         pltpu.make_async_remote_copy(
             src_ref=send_buf.at[target, chunk, pair, place, part],
             dst_ref=x_buf.at[chunk, pair, place, part, pl.ds(group * SLOTS, SLOTS), :],
-            send_sem=f_send, recv_sem=f_recv.at[2 * chunk + pair],
+            send_sem=f_send, recv_sem=f_recv.at[2 * pair + chunk],
             device_id=(ax, target), device_id_type=MESH,
         ).start()
 
@@ -186,7 +186,7 @@
     def send_rest(piece, carry):
         def send_more(count, carry):
             send_piece(
-                lax.div(piece, 4), lax.rem(lax.div(piece, 2), 2), lax.rem(piece, 2),
+                lax.rem(lax.div(piece, 2), 2), lax.div(piece, 4), lax.rem(piece, 2),
                 lax.rem(count * 5, 14),
             )
             return carry
@@ -341,36 +341,39 @@
             half * (NAZ // 2), (half + 1) * (NAZ // 2), add_alone, jnp.zeros((8, LANES), F32)
         )
 
-    def halo_copy(side):
+    def halo_copy(pair, side):
         return pltpu.make_async_remote_copy(
-            src_ref=halo_send.at[side], dst_ref=halo_recv.at[side],
-            send_sem=h_send.at[side], recv_sem=h_recv.at[side],
+            src_ref=halo_send.at[pair, side], dst_ref=halo_recv.at[pair, side],
+            send_sem=h_send.at[2 * pair + side], recv_sem=h_recv.at[2 * pair + side],
             device_id=(ax_target(1 if side == 0 else NAX - 1), az), device_id_type=MESH,
         )
 
-    def send_edges():
+    def send_edges(pair):
         def edges(block, carry):
             rows = pl.ds(pl.multiple_of(block * SLOTS, SLOTS), SLOTS)
             for side, lane in ((0, LANES - 1), (1, 0)):
                 tile = jnp.zeros((SLOTS, LANES), F32)
-                for c in range(4):
-                    tile = jnp.where(lane64 == c, fp[0, c, rows, lane : lane + 1], tile)
-                    tile = jnp.where(lane64 == 4 + c, fm[0, c, rows, lane : lane + 1], tile)
-                halo_send[side, rows, :] = tile
+                for place in range(2):
+                    field = pair + 2 * place
+                    tile = jnp.where(lane64 == place, fp[0, field, rows, lane : lane + 1], tile)
+                    tile = jnp.where(lane64 == 4 + place, fm[0, field, rows, lane : lane + 1], tile)
+                halo_send[pair, side, rows, :] = tile
             return carry
 
         lax.fori_loop(0, HALF // SLOTS, edges, 0)
         for side, lane in ((0, LANES - 1), (1, 0)):
             tile = jnp.zeros((8, LANES), F32)
-            for c in range(4):
-                tile = jnp.where(lane8 == c, fmid[0, c, :, lane : lane + 1], tile)
-            halo_send[side, pl.ds(HALF, 8), :] = tile
-        halo_copy(0).start()
-        halo_copy(1).start()
+            for place in range(2):
+                tile = jnp.where(
+                    lane8 == place, fmid[0, pair + 2 * place, :, lane : lane + 1], tile
+                )
+            halo_send[pair, side, pl.ds(HALF, 8), :] = tile
+        halo_copy(pair, 0).start()
+        halo_copy(pair, 1).start()
 
     def forward(unit, carry):
-        chunk = lax.div(unit, 2)
-        pair = lax.rem(unit, 2)
+        chunk = lax.rem(unit, 2)
+        pair = lax.div(unit, 2)
         arrived = x_buf.at[chunk, pair, :, :, pl.ds(0, 7 * SLOTS), :]
         pltpu.make_async_copy(arrived, arrived, f_recv.at[unit]).wait()
 
@@ -418,15 +421,15 @@
 
         lax.fori_loop(0, HALF // SLOTS, combine, 0)
 
-        @pl.when(unit == 1)
+        @pl.when(chunk == 0)
         def _():
-            send_edges()
-
-        return carry
-
-    lax.fori_loop(0, 3, forward, 0)
-    halo_copy(0).wait()
-    halo_copy(1).wait()
+            send_edges(pair)
+
+        return carry
+
+    lax.fori_loop(0, 2, forward, 0)
+    halo_copy(0, 0).wait()
+    halo_copy(0, 1).wait()
     left_on = jnp.where(ax > 0, 1.0, 0.0)
     right_on = jnp.where(ax < NAX - 1, 1.0, 0.0)
     here = inverse_radius(az)
@@ -464,17 +467,22 @@
 
         @pl.when(turn == 2)
         def _():
-            forward(3, 0)
+            lax.fori_loop(2, 4, forward, 0)
+            halo_copy(1, 0).wait()
+            halo_copy(1, 1).wait()
 
         def fluxes(block, sums):
             rows = pl.ds(pl.multiple_of(block * SLOTS, SLOTS), SLOTS)
             cell = lax.broadcasted_iota(jnp.int32, (SLOTS, CELLS), 1)
-            tile_l = halo_recv[0, rows, :]
-            tile_r = halo_recv[1, rows, :]
+            tile_l = halo_recv[0, 0, rows, :]
+            tile_r = halo_recv[0, 1, rows, :]
+            this_l = halo_recv[lax.rem(c, 2), 0, rows, :]
+            this_r = halo_recv[lax.rem(c, 2), 1, rows, :]
+            place = lax.div(c, 2)
             both = []
             for shift, source in ((0, fp), (4, fm)):
-                left = tile_l[:, shift : shift + 1] * pick_lane(tile_l, lane64, c + shift) * left_on
-                right = tile_r[:, shift : shift + 1] * pick_lane(tile_r, lane64, c + shift) * right_on
+                left = tile_l[:, shift : shift + 1] * pick_lane(this_l, lane64, place + shift) * left_on
+                right = tile_r[:, shift : shift + 1] * pick_lane(this_r, lane64, place + shift) * right_on
                 both.append(
                     flux_pair(
                         lambda chunk, field, source=source: source[chunk, field, rows, :],
@@ -494,13 +502,16 @@
             return sums + fold_rows(second * div_even)
 
         second_sum = lax.fori_loop(0, HALF // SLOTS, fluxes, jnp.zeros((8, CELLS), F32))
-        tile_l = halo_recv[0, pl.ds(HALF, 8), :]
-        tile_r = halo_recv[1, pl.ds(HALF, 8), :]
+        tile_l = halo_recv[0, 0, pl.ds(HALF, 8), :]
+        tile_r = halo_recv[0, 1, pl.ds(HALF, 8), :]
+        this_l = halo_recv[lax.rem(c, 2), 0, pl.ds(HALF, 8), :]
+        this_r = halo_recv[lax.rem(c, 2), 1, pl.ds(HALF, 8), :]
+        place = lax.div(c, 2)
         cell = lax.broadcasted_iota(jnp.int32, (8, CELLS), 1)
         div_mid, azi_mid = flux_pair(
             lambda chunk, field: fmid[chunk, field], None, c,
-            tile_l[:, 0:1] * pick_lane(tile_l, lane8, c) * left_on,
-            tile_r[:, 0:1] * pick_lane(tile_r, lane8, c) * right_on,
+            tile_l[:, 0:1] * pick_lane(this_l, lane8, place) * left_on,
+            tile_r[:, 0:1] * pick_lane(this_r, lane8, place) * right_on,
             cell,
         )
         div_mid = div_mid[0:1, :]
@@ -539,27 +550,89 @@
             for tile in range(2):
                 e_send[c, tile, part] = swept[:, tile * LANES : (tile + 1) * LANES]
         own_back(c).start()
-
-        def send_piece_back(piece, carry):
-            tile = 1 - lax.div(piece, 2)
-            part = lax.rem(piece, 2)
-
-            def send_back(offset, carry):
+        return carry
+
+    def field_of(turn):
+        return lax.rem(turn, 2) * 2 + lax.div(turn, 2)
+
+    def block_back(turn, tile, part, target, same):
+        c = field_of(turn)
+        pltpu.make_async_remote_copy(
+            src_ref=e_send.at[c, tile, part, pl.ds(lax.rem(target, 8) * SLOTS, SLOTS), :],
+            dst_ref=e_recv.at[c, tile, az, part],
+            send_sem=e_send_sem, recv_sem=e_recv_sem.at[same, 2 * c + tile],
+            device_id=(ax, target), device_id_type=MESH,
+        ).start()
+
+    def send_back(turn, tile):
+        def part_body(part, carry):
+            def body(count, carry):
+                index = lax.rem(count * 5, 12)
+                near = lax.div(index, 8)
+                same = lax.div(index, 9)
+                step = (1 - near) * (1 + 2 * lax.div(index, 4)) + (near - same) * 2
+                dy = (1 - near) * lax.rem(index, 4) + near * (index - 8)
+                block_back(turn, tile, part, column(step, dy), same)
+                return carry
+
+            return lax.fori_loop(0, 12, body, carry)
+
+        lax.fori_loop(0, 2, part_body, 0)
+
+    def send_back_direct(turn, tile):
+        def part_body(part, carry):
+            def body(offset, carry):
                 target = az_target(offset)
-                pltpu.make_async_remote_copy(
-                    src_ref=e_send.at[c, tile, part, pl.ds(lax.rem(target, 8) * SLOTS, SLOTS), :],
-                    dst_ref=e_recv.at[c, tile, az, part],
-                    send_sem=e_send_sem, recv_sem=e_recv_sem.at[2 * c + tile],
-                    device_id=(ax, target), device_id_type=MESH,
-                ).start()
+                step = lax.rem(lax.div(target, 4) + 4 - z, 4)
+                block_back(turn, tile, part, target, 1 - lax.div(step + 3, 4))
                 return carry
 
-            return lax.fori_loop(1, NAZ, send_back, carry)
-
-        lax.fori_loop(0, 4, send_piece_back, 0)
-        return carry
-
-    lax.fori_loop(0, FIELDS, explicit, 0)
+            return lax.fori_loop(1, NAZ, body, carry)
+
+        lax.fori_loop(0, 2, part_body, 0)
+
+    def same_landed(turn, tile):
+        c = field_of(turn)
+        ref = e_recv.at[c, tile, pl.ds(0, 3)]
+        pltpu.make_async_copy(ref, ref, e_recv_sem.at[1, 2 * c + tile]).wait()
+
+    def forward_on(turn, tile):
+        c = field_of(turn)
+        same_landed(turn, tile)
+
+        def body(count, carry):
+            block = e_recv.at[c, tile, column(0, 1 + lax.div(count, 2)), lax.rem(count, 2)]
+            pltpu.make_async_remote_copy(
+                src_ref=block, dst_ref=block,
+                send_sem=e_send_sem, recv_sem=e_recv_sem.at[0, 2 * c + tile],
+                device_id=(ax, column(2, 0)), device_id_type=MESH,
+            ).start()
+            return carry
+
+        lax.fori_loop(0, 6, body, 0)
+
+    def work(turn, carry):
+        explicit(turn, 0)
+
+        @pl.when(turn >= 2)
+        def _():
+            forward_on(turn - 2, 1)
+            forward_on(turn - 2, 0)
+
+        @pl.when(turn < 2)
+        def _():
+            send_back(turn, 1)
+            send_back(turn, 0)
+
+        @pl.when(turn == 2)
+        def _():
+            send_back_direct(turn, 1)
+            send_back_direct(turn, 0)
+
+        return carry
+
+    lax.fori_loop(0, FIELDS, work, 0)
+    send_back_direct(FIELDS - 1, 1)
 
     def state_sweep(radial, carry):
         build_transfer(radial, 1.0)
@@ -578,6 +651,7 @@
         st[radial] = swept.reshape(FIELDS, 2, SLOTS, CELLS)
         return carry
 
+    send_back_direct(FIELDS - 1, 0)
     lax.fori_loop(0, NR, state_sweep, 0)
 
     low_half = jnp.where(z < 2, 1.0, 0.0)
@@ -608,8 +682,12 @@
             return new_real, new_imag
 
         def landed(tile):
-            ref = e_recv.at[c, tile, pl.ds(0, NAZ - 1)]
-            pltpu.make_async_copy(ref, ref, e_recv_sem.at[2 * c + tile]).wait()
+            ref = e_recv.at[c, tile, pl.ds(0, NAZ - 4)]
+            pltpu.make_async_copy(ref, ref, e_recv_sem.at[0, 2 * c + tile]).wait()
+
+            @pl.when(turn >= 2)
+            def _():
+                same_landed(turn, tile)
 
         def add_last(radial, last):
             new_real, new_imag = add(1, radial)
@@ -710,8 +788,8 @@
             vmem((2, FIELDS, HALF, LANES), F32),
             vmem((2, FIELDS, HALF, LANES), F32),
             vmem((2, FIELDS, 8, LANES), F32),
-            vmem((2, HALF + 8, LANES), F32),
-            vmem((2, HALF + 8, LANES), F32),
+            vmem((2, 2, HALF + 8, LANES), F32),
+            vmem((2, 2, HALF + 8, LANES), F32),
             vmem((NR, CELLS), F32),
             vmem((CELLS, LANES), F32),
             vmem((CELLS, LANES), F32),
@@ -728,10 +806,10 @@
             dma,
             dma,
             dma,
-            dma((2,)),
-            dma((2,)),
+            dma((4,)),
+            dma((4,)),
             dma,
-            dma((2 * FIELDS,)),
+            dma((2, 2 * FIELDS)),
             dma((FIELDS,)),
             dma((FIELDS,)),
             dma,

time: 157 us -> 155 us (0.987)
  Pallas kernels: 151 us -> 149 us
    pallas_call x1, Pallas kernels: 151 us -> 149 us  [shards(): pl.pallas_call(kernel, out_shape=(jax.ShapeDtypeStruct((FIELDS, 2, NR, SL...]
where the time goes in v4:
time: 155 us
  Pallas kernels  149 us (96%)
  other arithmetic  6.21 us (4%)
    pallas_call x1, Pallas kernels, shards(): pl.pallas_call(kernel, out_shape=(jax.ShapeDtypeStruct((FIELDS, 2, NR, SL...  149 us
    add x1, other arithmetic, shards(): return acc + reach[None, None, :, None, :] * incoming_full[..., None]  6.21 us

profile of v4, /device:TPU:1, one launch (start us, length us, event | category | flops | bytes accessed | tf_op | source)
XLA Modules:
  0.0 155.2 jit_solution(1645526256618220003)
XLA Ops:
  0.0 149.0 %shard_map.46 = (f32[4,2,16,64,256]{4,3,2,1,0:T(8,128)}, f32[128,64]{1,0:T(8,128)}, f32[16,256]{1,0:T(8,128)}) custom-call(f32[4,2,16,64,256]{4,3,2,1,0:T(8,128)} %state_ref.1, f32[16,256]{1,0:T(8,128)} %courant_ref.1, s32[1,64]{1,0:T(1,128)} %bitcast.5, f32[128,64]{1,0:T(8,128)} %bitcast.3), custom_call_target="tpu_custom_call" | custom-call | tf_op jit(solution)/shard_map/pallas_call | solution.py:753
  149.0 6.2 %multiply_add_fusion = f32[4,2,16,64,256]{4,3,2,1,0:T(8,128)} fusion(f32[4,2,16,64,256]{4,3,2,1,0:T(8,128)} %get-tuple-element.8, f32[4,2,16,64]{3,2,1,0:T(8,128)} %bitcast.4, f32[16,256]{1,0:T(8,128)} %get-tuple-element.9), kind=kLoop, calls=%fused_computation | loop fusion | flops 4194304 | bytes 16826368 | tf_op jit(solution)/shard_map/add | solution.py:823

commit v5 on v4

--- a/solution.py
+++ b/solution.py
@@ -612,12 +612,17 @@
         lax.fori_loop(0, 6, body, 0)
 
     def work(turn, carry):
+        @pl.when(turn == 3)
+        def _():
+            forward_on(0, 1)
+            forward_on(0, 0)
+
         explicit(turn, 0)
 
-        @pl.when(turn >= 2)
+        @pl.when(turn == 3)
         def _():
-            forward_on(turn - 2, 1)
-            forward_on(turn - 2, 0)
+            forward_on(1, 1)
+            forward_on(1, 0)
 
         @pl.when(turn < 2)
         def _():

time: 155 us -> 155 us (level)
  no operation moved by 1% of the time
where the time goes in v5:
time: 155 us
  Pallas kernels  149 us (96%)
  other arithmetic  6.21 us (4%)
    pallas_call x1, Pallas kernels, shards(): pl.pallas_call(kernel, out_shape=(jax.ShapeDtypeStruct((FIELDS, 2, NR, SL...  149 us
    add x1, other arithmetic, shards(): return acc + reach[None, None, :, None, :] * incoming_full[..., None]  6.21 us

profile of v5, /device:TPU:1, one launch (start us, length us, event | category | flops | bytes accessed | tf_op | source)
XLA Modules:
  0.0 155.3 jit_solution(6553153136583219125)
XLA Ops:
  0.0 149.0 %shard_map.46 = (f32[4,2,16,64,256]{4,3,2,1,0:T(8,128)}, f32[128,64]{1,0:T(8,128)}, f32[16,256]{1,0:T(8,128)}) custom-call(f32[4,2,16,64,256]{4,3,2,1,0:T(8,128)} %state_ref.1, f32[16,256]{1,0:T(8,128)} %courant_ref.1, s32[1,64]{1,0:T(1,128)} %bitcast.5, f32[128,64]{1,0:T(8,128)} %bitcast.3), custom_call_target="tpu_custom_call" | custom-call | tf_op jit(solution)/shard_map/pallas_call | solution.py:758
  149.1 6.2 %multiply_add_fusion = f32[4,2,16,64,256]{4,3,2,1,0:T(8,128)} fusion(f32[4,2,16,64,256]{4,3,2,1,0:T(8,128)} %get-tuple-element.8, f32[4,2,16,64]{3,2,1,0:T(8,128)} %bitcast.4, f32[16,256]{1,0:T(8,128)} %get-tuple-element.9), kind=kLoop, calls=%fused_computation | loop fusion | flops 4194304 | bytes 16826368 | tf_op jit(solution)/shard_map/add | solution.py:828
